TPU v7x, 512 devices: a whole 4x8x8 slice. The times are simulated.
512 devices in a mesh: dp: 128 (over z_lo, x, y), slab: 4 (over z_hi, core).
Axes of the slice: x: 4, y: 8, z: 8 (z_hi: 2, z_lo: 4; z = z_hi * 4 + z_lo), core: 2. Of those that a mesh axis runs over, the one named last changes fastest.
Arguments:
- features: bfloat16 [128, 48, 40, 2048], P('dp', 'slab'), may hold values from -6 to 6
- labels: int32 [128, 48, 40], P('dp', 'slab'), may hold values from 0 to 2
- cotangent: bfloat16 [128, 48, 40, 256], P('dp', 'slab'), may hold values from -6 to 6
- first_kernel: float32 [3, 3, 2048], replicated, may hold values from -2 to 2
- holed_kernel: float32 [3, 3, 2048], replicated, may hold values from -2 to 2
- point_weight: bfloat16 [2048, 256], replicated, may hold values from -0.125 to 0.125
Outputs:
- branch_out: bfloat16 [128, 48, 40, 256], P('dp', 'slab')
- point_grad: bfloat16 [2048, 256], replicated
- first_grad: float32 [3, 3, 2048], replicated
- atrous_grad: float32 [3, 3, 2048], replicated
All inputs are finite; a program needn't handle non-finite values.
Results may differ from a plain program's by a relative error of at most 0.015.
Values may be sent and summed in bfloat16 or wider, within the bound.
No kernel may reach another device: no remote copies, remote signals or barrier semaphores. Data moves between devices by JAX's collectives and lax.ppermute only.
A program may use at most 128 MiB of HBM per device.

v0:
```python
import math

import jax
import jax.numpy as jnp
from jax import lax
from jax.sharding import PartitionSpec as P

DILATION_STEP = 36


def from_behind(value, axis, steps):
    count = lax.axis_size(axis)
    initial, last = (max(0, -steps), min(count, count - steps))
    return lax.ppermute(value, axis, [(source, source + steps) for source in range(initial, last)])


def extended(block, sides, width):
    for axis, dim in sides:
        count = lax.axis_size(axis)
        forward = [(i, i + 1) for i in range(count - 1)]
        backward = [(target, source) for source, target in forward]
        low = lax.ppermute(
            lax.slice_in_dim(block, block.shape[dim] - width, None, axis=dim), axis, forward
        )
        high = lax.ppermute(lax.slice_in_dim(block, 0, width, axis=dim), axis, backward)
        block = jnp.concatenate([low, block, high], axis=dim)
    return block


def class_weighting(labels):
    return jnp.where(labels == 0, 0.6, jnp.where(labels == 1, 2.4, 1.5)).astype(jnp.float32)


def kernel_tap_window(padded, kernel, row_count, column_count, stride):
    summed = jnp.zeros((row_count, column_count, padded.shape[2]), jnp.float32)
    for row_tap in range(3):
        for col_tap in range(3):
            window = padded[
                row_tap * stride : row_tap * stride + row_count,
                col_tap * stride : col_tap * stride + column_count,
            ]
            summed = summed + kernel[row_tap, col_tap] * window
    return summed


def kernel_tap_product(padded, gradient, row_count, column_count, stride):
    pieces = []
    for row_tap in range(3):
        for col_tap in range(3):
            window = padded[
                row_tap * stride : row_tap * stride + row_count,
                col_tap * stride : col_tap * stride + column_count,
            ]
            pieces.append(jnp.sum(window * gradient, axis=(0, 1)))
    return jnp.stack(pieces).reshape(3, 3, -1)


def widen_cols(slab_block, stride):
    return jnp.pad(slab_block[0].astype(jnp.float32), ((0, 0), (stride, stride), (0, 0)))


def holed_rows(blocks, kernel, column_count, stride):
    summed = jnp.zeros(blocks[1].shape[1:], jnp.float32)
    for row_tap in range(3):
        widened = widen_cols(blocks[row_tap], stride)
        for col_tap in range(3):
            summed = (
                summed
                + kernel[row_tap, col_tap]
                * widened[:, col_tap * stride : col_tap * stride + column_count]
            )
    return summed


def holed_multiply(blocks, gradient, column_count, stride):
    pieces = []
    for row_tap in range(3):
        widened = widen_cols(blocks[row_tap], stride)
        for col_tap in range(3):
            window = widened[:, col_tap * stride : col_tap * stride + column_count]
            pieces.append(jnp.sum(window * gradient, axis=(0, 1)))
    return jnp.stack(pieces).reshape(3, 3, -1)


def far_rows(slab_block):
    halo_extent = DILATION_STEP // slab_block.shape[1]
    from_above = from_behind(slab_block, "slab", halo_extent)
    from_below = from_behind(slab_block, "slab", -halo_extent)
    return (from_above, from_below)


def per_device(features, labels, cotangent, first_kernel, holed_kernel, point_weight):
    row_count = features.shape[1]
    column_count = features.shape[2]
    channels = features.shape[3]
    out_width = point_weight.shape[1]
    reversed_kernel = holed_kernel[::-1, ::-1]
    scale_factor = 1.0 / math.sqrt(
        lax.axis_size("dp") * lax.axis_size("slab") * row_count * column_count
    )
    weighting = class_weighting(labels[0])[:, :, None]
    weighted = (cotangent[0].astype(jnp.float32) * weighting).astype(jnp.bfloat16)
    weighted_flat = weighted.reshape(row_count * column_count, out_width)
    bordered = extended(features, (("slab", 1),), 1)
    padded_in = jnp.pad(bordered[0].astype(jnp.float32), ((0, 0), (1, 1), (0, 0)))
    first = kernel_tap_window(padded_in, first_kernel, row_count, column_count, 1).astype(
        jnp.bfloat16
    )[None]
    first_above, first_below = far_rows(first)
    leading_blocks = (first_above, first, first_below)
    holed_output = holed_rows(leading_blocks, holed_kernel, column_count, DILATION_STEP).astype(
        jnp.bfloat16
    )[None]
    atrous_flat = holed_output.reshape(row_count * column_count, channels)
    branch_out = jnp.dot(atrous_flat, point_weight, preferred_element_type=jnp.float32).astype(
        jnp.bfloat16
    )
    branch_out = branch_out.reshape(1, row_count, column_count, out_width)
    holed_gradient = lax.dot_general(
        weighted_flat, point_weight, (((1,), (1,)), ((), ())), preferred_element_type=jnp.float32
    ).astype(jnp.bfloat16)
    point_part = lax.dot_general(
        atrous_flat, weighted_flat, (((0,), (0,)), ((), ())), preferred_element_type=jnp.float32
    )
    holed_gradient = holed_gradient.reshape(1, row_count, column_count, channels)
    gradient_widened = holed_gradient[0].astype(jnp.float32)
    gradient_upper_halo, gradient_lower_halo = far_rows(holed_gradient)
    holed_portion = holed_multiply(leading_blocks, gradient_widened, column_count, DILATION_STEP)
    leading_gradient = holed_rows(
        (gradient_upper_halo, holed_gradient, gradient_lower_halo),
        reversed_kernel,
        column_count,
        DILATION_STEP,
    ).astype(jnp.bfloat16)
    first_part = kernel_tap_product(
        padded_in, leading_gradient.astype(jnp.float32), row_count, column_count, 1
    )
    point_sum, first_sum, holed_total_sum = lax.psum(
        (point_part, first_part, holed_portion), ("dp", "slab")
    )
    point_grad = (point_sum * scale_factor).astype(jnp.bfloat16)
    return (branch_out, point_grad, first_sum * scale_factor, holed_total_sum * scale_factor)


def solution(mesh):
    in_specs = (
        P("dp", "slab", None, None),
        P("dp", "slab", None),
        P("dp", "slab", None, None),
        P(),
        P(),
        P(),
    )
    out_specs = (P("dp", "slab", None, None), P(), P(), P())
    return jax.shard_map(
        per_device, mesh=mesh, in_specs=in_specs, out_specs=out_specs, check_vma=False
    )
```

profile of v0, /device:TPU:1, one launch (start us, length us, event | category | flops | bytes accessed | tf_op | source)
XLA Modules:
  0.0 423.7 jit_solution(1523050457168167211)
XLA Ops:
  7.2 0.0 copy-start
  7.2 0.0 copy-start.6
  7.2 0.0 copy-start.7
  7.2 0.0 all-reduce.10.cloned.1.call-start
  7.2 0.8 fusion.39
  8.1 0.1 select_n.29
  8.1 0.0 copy-start.3
  8.2 1.2 fusion.33
  9.4 0.0 copy-done
  9.4 0.7 convolution_convert_fusion
  10.1 1.9 collective-permute-start.5
  12.1 1.9 collective-permute-start.4
  14.0 12.0 %collective-permute-start = (bf16[1,1,40,2048]{3,2,1,0:T(8,128)(2,1)S(1)}, bf16[1,1,40,2048]{3,2,1,0:T(8,128)(2,1)S(1)}, u32[]{:S(2)}, u32[]{:S(2)}) collective-permute-start(bf16[1,1,40,2048]{3,2,1,0:T(8,128)(2,1)S(1)} %get-tuple-element.38), channel_id=1, source_target_pairs={{0,1},{1,2},{2,3},{4,5},{5,6},{6,7},{8,9},{9,10},{10,11},{12,13},{... | collective-permute-start | bytes 491528 | tf_op jit(solution)/shard_map/ppermute | solution.py:22
  26.0 6.2 %collective-permute-start.1 = (bf16[1,1,40,2048]{3,2,1,0:T(8,128)(2,1)S(1)}, bf16[1,1,40,2048]{3,2,1,0:T(8,128)(2,1)S(1)}, u32[]{:S(2)}, u32[]{:S(2)}) collective-permute-start(bf16[1,1,40,2048]{3,2,1,0:T(8,128)(2,1)S(1)} %get-tuple-element.39), channel_id=1, source_target_pairs={{1,0},{2,1},{3,2},{5,4},{6,5},{7,6},{9,8},{10,9},{11,10},{13,12},{... | collective-permute-start | bytes 491528 | tf_op jit(solution)/shard_map/ppermute | solution.py:25
  32.3 0.1 fusion.43
  32.3 0.1 fusion.42
  32.4 2.4 convert.10
  34.8 0.0 collective-permute-done
  34.8 5.6 %collective-permute-done.1 = bf16[1,1,40,2048]{3,2,1,0:T(8,128)(2,1)S(1)} collective-permute-done((bf16[1,1,40,2048]{3,2,1,0:T(8,128)(2,1)S(1)}, bf16[1,1,40,2048]{3,2,1,0:T(8,128)(2,1)S(1)}, u32[]{:S(2)}, u32[]{:S(2)}) %collective-permute-start.1) | collective-permute-done | bytes 163872 | tf_op jit(solution)/shard_map/ppermute | solution.py:25
  40.4 2.6 fusion.38
  43.0 13.2 %fusion.40 = (f32[12,40,2048]{2,1,0:T(8,128)}, bf16[12,40,2048]{2,1,0:T(8,128)(2,1)}) fusion(f32[2048]{0:T(1024)S(1)} %bitcast.133, f32[1,14,40,2048]{3,2,1,0:T(8,128)S(1)} %get-tuple-element.37, f32[2048]{0:T(1024)S(1)} %bitcast.134, f32[2048]{0:T(1024)S(1)} %bitcast.127, f32[2048]{0:T(1024)S(1)} %bitcast.128, f32[2048]{0:T(1024)S(1)} %bitcast.129, ...), kind=kLoop, calls=%fused_computation.97 | loop fusion | flops 18677760 | bytes 22355968 | tf_op jit(solution)/shard_map/convert_element_type | solution.py:59
  56.2 2.0 collective-permute-start.3
  58.2 2.0 collective-permute-start.2
  60.2 0.0 collective-permute-done.5
  60.2 3.9 bitcast_convert_fusion
  64.1 0.0 collective-permute-done.4
  64.1 3.9 bitcast_convert_fusion.1
  68.0 16.6 %fusion.23 = (f32[2048]{0:T(1024)S(1)}, f32[2048]{0:T(1024)S(1)}, f32[2048]{0:T(1024)S(1)}, f32[2048]{0:T(1024)S(1)}, f32[2048]{0:T(1024)S(1)}, /*index=5*/f32[2...) fusion(f32[14,40,2048]{2,1,0:T(8,128)} %get-tuple-element.36, ...), kind=kLoop, calls=%fused_computation.60 | loop fusion | flops 37337088 | bytes 30294016 | tf_op jit(solution)/shard_map/reduce_sum | solution.py:54
  84.7 0.1 stack.69
  84.8 0.7 reshape.75
  85.5 0.0 collective-permute-done.2
  85.5 2.0 bitcast_convert_fusion.3
  87.5 0.0 collective-permute-done.3
  87.5 2.2 bitcast_convert_fusion.2
  89.7 0.5 copy-done.1
  90.2 3.3 add_convert_fusion
  93.5 0.0 copy-done.2
  93.5 4.6 %fusion.14 = (f32[2048]{0:T(1024)S(1)}, f32[2048]{0:T(1024)S(1)}, f32[2048]{0:T(1024)S(1)}, f32[2048]{0:T(1024)S(1)}, f32[2048]{0:T(1024)S(1)}, /*index=5*/f32[2...) fusion(bf16[12,40,2048]{2,1,0:T(8,128)(2,1)S(1)} %bitcast.104, ...), kind=kLoop, calls=%fused_computation.51 | loop fusion | flops 21608448 | bytes 19734528 | tf_op jit(solution)/shard_map/reduce_sum | solution.py:81
  98.1 0.1 stack.79
  98.2 0.7 reshape.76
  98.9 0.0 copy-done.5
  98.9 3.8 convolution_bitcast_fusion
  102.8 0.0 all-reduce.10.cloned.1.call-update
  102.8 0.0 copy-done.4
  102.8 1.4 convolution_convert_fusion.1
  104.2 308.2 %all-reduce.10.cloned.1.call-done = (f32[2048,256]{1,0:T(8,128)}, f32[3,3,2048]{2,1,0:T(4,128)}, f32[3,3,2048]{2,1,0:T(4,128)}) async-done(((f32[2048,256]{1,0:T(8,128)}, f32[3,3,2048]{2,1,0:T(4,128)}, f32[3,3,2048]{2,1,0:T(4,128)}), (f32[2048,256]{1,0:T(8,128)}, f32[3,3,2048]{2,1,0:T(4,128)}, f32[3,3,2048]{2,1,0:T(4,128)})) %all-reduce.10.cloned.1.call-update) | async-done | bytes 2244624 | tf_op jit(solution)/shard_map/psum | solution.py:138
  412.4 2.8 multiply_convert_fusion
  415.2 1.7 broadcast_multiply_fusion
  (9 shorter events, 0.0 us)
Async XLA Ops:
  7.2 2.2 copy-start
  7.2 25.1 %copy-start.6 = (f32[3,3,2048]{2,1,0:T(4,128)S(1)}, f32[3,3,2048]{2,1,0:T(4,128)}, u32[]{:S(2)}) copy-start(f32[3,3,2048]{2,1,0:T(4,128)} %param.9) | copy-start | bytes 221188
  7.2 25.1 %copy-start.7 = (f32[3,3,2048]{2,1,0:T(4,128)S(1)}, f32[3,3,2048]{2,1,0:T(4,128)}, u32[]{:S(2)}) copy-start(f32[3,3,2048]{2,1,0:T(4,128)} %param.10) | copy-start | bytes 221188
  7.2 405.2 %all-reduce.10.cloned.1.call-start = ((), (), s32[]{:S(2)}) async-start(), calls=%async_computation | async-start | bytes 4587520 | tf_op jit(solution)/shard_map/psum | solution.py:138
  8.1 5.8 %copy-start.3 = (bf16[1,12,40,2048]{3,2,1,0:T(8,128)(2,1)S(1)}, bf16[1,12,40,2048]{3,2,1,0:T(8,128)(2,1)}, u32[]{:S(2)}) copy-start(bf16[1,12,40,2048]{3,2,1,0:T(8,128)(2,1)} %param.6) | copy-start | bytes 5898244
  10.1 50.1 %collective-permute-start.5 = (bf16[1,12,40,2048]{3,2,1,0:T(8,128)(2,1)S(1)}, bf16[1,12,40,2048]{3,2,1,0:T(8,128)(2,1)}, u32[]{:S(2)}, u32[]{:S(2)}) collective-permute-start(bf16[1,12,40,2048]{3,2,1,0:T(8,128)(2,1)S(1)} %bitcast.100), channel_id=1, source_target_pairs={{3,0},{7,4},{11,8},{15,12},{19,16},{23,20},{27,24},{31,28},{35,32}... | collective-permute-start | bytes 5898248 | tf_op jit(solution)/shard_map/ppermute | solution.py:14
  12.1 52.1 %collective-permute-start.4 = (bf16[1,12,40,2048]{3,2,1,0:T(8,128)(2,1)S(1)}, bf16[1,12,40,2048]{3,2,1,0:T(8,128)(2,1)}, u32[]{:S(2)}, u32[]{:S(2)}) collective-permute-start(bf16[1,12,40,2048]{3,2,1,0:T(8,128)(2,1)S(1)} %bitcast.101), channel_id=1, source_target_pairs={{0,3},{4,7},{8,11},{12,15},{16,19},{20,23},{24,27},{28,31},{32,35}... | collective-permute-start | bytes 5898248 | tf_op jit(solution)/shard_map/ppermute | solution.py:14
  14.0 20.8 %collective-permute-start = (bf16[1,1,40,2048]{3,2,1,0:T(8,128)(2,1)S(1)}, bf16[1,1,40,2048]{3,2,1,0:T(8,128)(2,1)S(1)}, u32[]{:S(2)}, u32[]{:S(2)}) collective-permute-start(bf16[1,1,40,2048]{3,2,1,0:T(8,128)(2,1)S(1)} %get-tuple-element.38), channel_id=1, source_target_pairs={{0,1},{1,2},{2,3},{4,5},{5,6},{6,7},{8,9},{9,10},{10,11},{12,13},{... | collective-permute-start | bytes 491528 | tf_op jit(solution)/shard_map/ppermute | solution.py:22
  26.0 14.3 %collective-permute-start.1 = (bf16[1,1,40,2048]{3,2,1,0:T(8,128)(2,1)S(1)}, bf16[1,1,40,2048]{3,2,1,0:T(8,128)(2,1)S(1)}, u32[]{:S(2)}, u32[]{:S(2)}) collective-permute-start(bf16[1,1,40,2048]{3,2,1,0:T(8,128)(2,1)S(1)} %get-tuple-element.39), channel_id=1, source_target_pairs={{1,0},{2,1},{3,2},{5,4},{6,5},{7,6},{9,8},{10,9},{11,10},{13,12},{... | collective-permute-start | bytes 491528 | tf_op jit(solution)/shard_map/ppermute | solution.py:25
  56.2 31.3 %collective-permute-start.3 = (bf16[1,12,40,2048]{3,2,1,0:T(8,128)(2,1)}, bf16[1,12,40,2048]{3,2,1,0:T(8,128)(2,1)}, u32[]{:S(2)}, u32[]{:S(2)}) collective-permute-start(bf16[1,12,40,2048]{3,2,1,0:T(8,128)(2,1)} %bitcast.105), channel_id=1, source_target_pairs={{3,0},{7,4},{11,8},{15,12},{19,16},{23,20},{27,24},{31,28},{35,32}... | collective-permute-start | bytes 5898248 | tf_op jit(solution)/shard_map/ppermute | solution.py:14
  58.2 27.3 %collective-permute-start.2 = (bf16[1,12,40,2048]{3,2,1,0:T(8,128)(2,1)}, bf16[1,12,40,2048]{3,2,1,0:T(8,128)(2,1)}, u32[]{:S(2)}, u32[]{:S(2)}) collective-permute-start(bf16[1,12,40,2048]{3,2,1,0:T(8,128)(2,1)} %bitcast.106), channel_id=1, source_target_pairs={{0,3},{4,7},{8,11},{12,15},{16,19},{20,23},{24,27},{28,31},{32,35}... | collective-permute-start | bytes 5898248 | tf_op jit(solution)/shard_map/ppermute | solution.py:14
  87.5 2.7 copy-start.1
  90.2 3.3 copy-start.2
  93.5 5.4 %copy-start.5 = (bf16[1,12,40,256]{3,2,1,0:T(8,128)(2,1)S(1)}, bf16[1,12,40,256]{3,2,1,0:T(8,128)(2,1)}, u32[]{:S(2)}) copy-start(bf16[1,12,40,256]{3,2,1,0:T(8,128)(2,1)} %param.8) | copy-start | bytes 737284
  98.9 3.9 copy-start.4
Sparse Core Ops, SparseCore 0:
  102.9 309.4 all-reduce.9
where the time goes:
time: 425 us; the launch traced here: 424 us
  waiting for transfers between devices  314 us (74%)
  other arithmetic  61.2 us (14%)
  starting transfers between devices  26.1 us (6%)
  between operations  14.2 us (3%)
  matrix products  5.93 us (1%)
    psum x1, waiting for transfers between devices, per_device(): lax.psum((point_part, first_part, holed_portion), ('dp', 'slab'))  308 us
    convert_element_type x6, other arithmetic, widen_cols(): slab_block[0].astype(jnp.float32)  27.6 us
    reduce_sum x1, other arithmetic, kernel_tap_product(): pieces.append(jnp.sum(window * gradient, axis=(0, 1)))  16.6 us
    ppermute x1, starting transfers between devices, extended(): lax.ppermute(lax.slice_in_dim(block, block.shape[dim] - width, None, axis...  12 us
  transfers between devices with their start and end apart: 7, of which 2 were waited for; matrix products, arithmetic and copies ran while one was open for 11% of the time, Pallas kernels for 0%

commit v1 on v0

v1 whole, which is shorter than its diff:
```python
import itertools
import math

import jax
import jax.numpy as jnp
from jax import lax
from jax.experimental import pallas as pl
from jax.experimental.pallas import tpu as pltpu
from jax.sharding import PartitionSpec as P

AXES = ("dp", "slab")
STEP = 36
ROWS = 12
COLS = 40
CELLS = ROWS * COLS
EDGE = COLS - STEP
CHANNELS = 2048
WIDTH = 256
BLOCK = 256
LANES = 128
GRAD_ROWS = 32
PAYLOAD_ROWS = 2 * CHANNELS + CHANNELS // LANES * GRAD_ROWS
F32 = jnp.float32
BF16 = jnp.bfloat16


def device_groups(dims, *names):
    strides, stride = {}, 1
    for name in reversed(dims):
        strides[name] = stride
        stride *= dims[name]

    def places(chosen):
        return [
            sum(i * strides[n] for n, i in zip(chosen, spot))
            for spot in itertools.product(*(range(dims[n]) for n in chosen))
        ]

    inside = places(names)
    return [[base + i for i in inside] for base in places([n for n in dims if n not in names])]


def exchange(parts, groups):
    return lax.all_to_all(parts, AXES, 0, 0, axis_index_groups=groups, tiled=True)


def scattered(units, groups):
    count = len(groups[0])
    parts = exchange(units.reshape(count, units.shape[0] // count, 8, LANES), groups)
    return jnp.sum(parts.astype(F32), axis=0)


def gathered(units, groups):
    count = len(groups[0])
    return exchange(jnp.broadcast_to(units[None], (count, *units.shape)), groups)


def body(
    slab_ref,
    x_ref,
    near_ref,
    far_ref,
    weighted_ref,
    partner_ref,
    first_k_ref,
    holed_k_ref,
    point_ref,
    payload_ref,
    own_out_ref,
    far_out_ref,
    xs,
    wfar,
    b_own,
    b_far,
    a_own,
    a_far,
    own_acc,
    far_acc,
):
    step = pl.program_id(0)
    slab = slab_ref[0]
    core = lax.rem(slab, 2)
    outer = jnp.logical_or(slab == 0, slab == 3)

    @pl.when(step == 0)
    def _():
        keep = jnp.where(outer, 1.0, 0.0)
        wfar[...] = (partner_ref[...].astype(F32) * keep).astype(BF16)
        own_acc[...] = jnp.zeros_like(own_acc)
        far_acc[...] = jnp.zeros_like(far_acc)

    near = near_ref[...].astype(F32)
    far = far_ref[...].astype(F32)
    is_one = jnp.where(core == 1, 1.0, 0.0)
    is_zero = 1.0 - is_one
    xs[pl.ds(0, COLS), :] = near * is_one + far * jnp.where(slab == 2, 1.0, 0.0)
    xs[pl.ds((ROWS + 1) * COLS, COLS), :] = near * is_zero + far * jnp.where(slab == 1, 1.0, 0.0)

    def widen(r, _):
        xs[pl.ds(pl.multiple_of((r + 1) * COLS, 8), COLS), :] = x_ref[r].astype(F32)
        return 0

    lax.fori_loop(0, ROWS, widen, 0)

    weights = point_ref[...]
    nt = (((1,), (1,)), ((), ()))
    tn = (((0,), (0,)), ((), ()))
    b_own[...] = (
        lax.dot_general(weighted_ref[...], weights, nt, preferred_element_type=F32)
        .astype(BF16)
        .astype(F32)
    )
    b_far[...] = (
        lax.dot_general(wfar[...], weights, nt, preferred_element_type=F32)
        .astype(BF16)
        .astype(F32)
    )

    col = lax.broadcasted_iota(jnp.int32, (COLS, LANES), 0)
    sub = lax.broadcasted_iota(jnp.int32, (8, LANES), 0)
    low = sub < EDGE
    up_f = jnp.where(slab == 0, 1.0, 0.0)
    down_f = jnp.where(slab == 3, 1.0, 0.0)

    def from_left(v):
        return jnp.where(col == 0, 0.0, pltpu.roll(v, 1, 0))

    def from_right(v):
        return jnp.where(col == COLS - 1, 0.0, pltpu.roll(v, COLS - 1, 0))

    def fold(v):
        parts = [v[8 * i : 8 * i + 8] for i in range(COLS // 8)]
        while len(parts) > 1:
            parts = [a + b for a, b in zip(parts[::2], parts[1::2])] + (
                parts[-1:] if len(parts) % 2 else []
            )
        return parts[0]

    for chunk in range(BLOCK // LANES):
        lanes = pl.ds(chunk * LANES, LANES)
        fk = [[first_k_ref[i, j : j + 1, lanes] for j in range(3)] for i in range(3)]
        hk = [[holed_k_ref[i, j : j + 1, lanes] for j in range(3)] for i in range(3)]
        mk = hk[1]
        kf = [hk[0][j] * up_f + hk[2][j] * down_f for j in range(3)]

        def pair(p, acc, lanes=lanes, fk=fk, mk=mk, kf=kf):
            first_acc, own_g, far_g = [list(a) for a in acc]
            base = pl.multiple_of(p * 2 * COLS, 2 * COLS)
            x = [xs[pl.ds(pl.multiple_of(base + i * COLS, 8), COLS), lanes] for i in range(4)]
            own_rows, far_rows = [], []
            for r in range(2):
                side = [
                    fk[0][j] * x[r] + fk[1][j] * x[r + 1] + fk[2][j] * x[r + 2] for j in range(3)
                ]
                f = side[1] + from_left(side[0]) + from_right(side[2])
                f = f.astype(BF16).astype(F32)
                here = pl.ds(pl.multiple_of(base + r * COLS, 8), COLS)
                bo, bf = b_own[here, lanes], b_far[here, lanes]
                f_hi = jnp.where(low, pltpu.roll(f[STEP - EDGE :], 4, 0), 0.0)
                f_lo = jnp.where(low, 0.0, pltpu.roll(f[:8], 4, 0))

                def spread(k, v, v_hi, v_lo, left, right):
                    c = k * v
                    return jnp.concatenate(
                        [c[:8] + right * v_hi, c[8 : COLS - 8], c[COLS - 8 :] + left * v_lo], 0
                    )

                own_rows.append(spread(mk[1], f, f_hi, f_lo, mk[0], mk[2]))
                far_rows.append(spread(kf[1], f, f_hi, f_lo, kf[0], kf[2]))
                own_g[0] += f_lo * bo[COLS - 8 :]
                own_g[1] += fold(f * bo)
                own_g[2] += f_hi * bo[:8]
                far_g[0] += f_lo * bf[COLS - 8 :]
                far_g[1] += fold(f * bf)
                far_g[2] += f_hi * bf[:8]
                bo_hi = pltpu.roll(bo[COLS - 8 :], 4, 0)
                bo_lo = pltpu.roll(bo[:8], 4, 0)
                bf_hi = pltpu.roll(bf[COLS - 8 :], 4, 0)
                bf_lo = pltpu.roll(bf[:8], 4, 0)
                g = mk[1] * bo + kf[1] * bf
                g_hi = jnp.where(low, mk[0] * bo_hi + kf[0] * bf_hi, 0.0)
                g_lo = jnp.where(low, 0.0, mk[2] * bo_lo + kf[2] * bf_lo)
                g = jnp.concatenate([g[:8] + g_hi, g[8 : COLS - 8], g[COLS - 8 :] + g_lo], 0)
                g = g.astype(BF16).astype(F32)
                shifted = [from_right(g), g, from_left(g)]
                for i in range(3):
                    for j in range(3):
                        first_acc[3 * i + j] += fold(x[r + i] * shifted[j])
            there = pl.ds(base, 2 * COLS)
            a_own[there, lanes] = jnp.concatenate(own_rows, 0).astype(BF16)
            a_far[there, lanes] = jnp.concatenate(far_rows, 0).astype(BF16)
            return tuple(first_acc), tuple(own_g), tuple(far_g)

        zero = jnp.zeros((8, LANES), F32)
        first_acc, own_g, far_g = lax.fori_loop(
            0, ROWS // 2, pair, ((zero,) * 9, (zero,) * 3, (zero,) * 3)
        )

        def line(v):
            return jnp.sum(v, axis=0, keepdims=True)

        far_lines = [line(v) for v in far_g]
        lines = [line(v) for v in first_acc]
        lines += [v * up_f for v in far_lines]
        lines += [line(v) for v in own_g]
        lines += [v * down_f for v in far_lines]
        lines.append(jnp.zeros((GRAD_ROWS - len(lines), LANES), F32))
        at = 2 * CHANNELS + (step * (BLOCK // LANES) + chunk) * GRAD_ROWS
        payload_ref[pl.ds(pl.multiple_of(at, GRAD_ROWS), GRAD_ROWS), :] = jnp.concatenate(
            lines, 0
        ).astype(BF16)

    own_acc[...] += jnp.dot(a_own[...], weights, preferred_element_type=F32)
    far_acc[...] += jnp.dot(a_far[...], weights, preferred_element_type=F32)
    part = lax.dot_general(a_own[...], weighted_ref[...], tn, preferred_element_type=F32)
    part += lax.dot_general(a_far[...], wfar[...], tn, preferred_element_type=F32)
    for half in range(WIDTH // LANES):
        at = pl.multiple_of(half * CHANNELS + step * BLOCK, BLOCK)
        payload_ref[pl.ds(at, BLOCK), :] = part[:, half * LANES : (half + 1) * LANES].astype(BF16)

    @pl.when(step == pl.num_programs(0) - 1)
    def _():
        own_out_ref[...] = own_acc[...]
        far_out_ref[...] = far_acc[...].astype(BF16)


def slab_work(slab, features, near, partner, weighted, first_kernel, holed_kernel, point_weight):
    whole = lambda shape: pl.BlockSpec(shape, lambda k, s: (0,) * len(shape))
    return pl.pallas_call(
        body,
        grid_spec=pltpu.PrefetchScalarGridSpec(
            num_scalar_prefetch=1,
            grid=(CHANNELS // BLOCK,),
            in_specs=[
                pl.BlockSpec((ROWS, COLS, BLOCK), lambda k, s: (0, 0, k)),
                pl.BlockSpec((COLS, BLOCK), lambda k, s: (0, k)),
                pl.BlockSpec((COLS, BLOCK), lambda k, s: (k, 0)),
                whole((CELLS, WIDTH)),
                whole((CELLS, WIDTH)),
                pl.BlockSpec((3, 3, BLOCK), lambda k, s: (0, 0, k)),
                pl.BlockSpec((3, 3, BLOCK), lambda k, s: (0, 0, k)),
                pl.BlockSpec((BLOCK, WIDTH), lambda k, s: (k, 0)),
            ],
            out_specs=[
                whole((PAYLOAD_ROWS, LANES)),
                whole((CELLS, WIDTH)),
                whole((CELLS, WIDTH)),
            ],
            scratch_shapes=[
                pltpu.VMEM(((ROWS + 2) * COLS, BLOCK), F32),
                pltpu.VMEM((CELLS, WIDTH), BF16),
                pltpu.VMEM((CELLS, BLOCK), F32),
                pltpu.VMEM((CELLS, BLOCK), F32),
                pltpu.VMEM((CELLS, BLOCK), BF16),
                pltpu.VMEM((CELLS, BLOCK), BF16),
                pltpu.VMEM((CELLS, WIDTH), F32),
                pltpu.VMEM((CELLS, WIDTH), F32),
            ],
        ),
        out_shape=[
            jax.ShapeDtypeStruct((PAYLOAD_ROWS, LANES), BF16),
            jax.ShapeDtypeStruct((CELLS, WIDTH), F32),
            jax.ShapeDtypeStruct((CELLS, WIDTH), BF16),
        ],
        compiler_params=pltpu.CompilerParams(vmem_limit_bytes=40 * 2**20),
        cost_estimate=pl.CostEstimate(
            flops=6 * 2 * CELLS * CHANNELS * WIDTH, bytes_accessed=6 * 2**20, transcendentals=0
        ),
    )(slab, features, near, partner, weighted, partner, first_kernel, holed_kernel, point_weight)


def per_device(features, labels, cotangent, first_kernel, holed_kernel, point_weight):
    count = lax.axis_size("dp")
    dims = {"z_lo": 4, "x": 4, "y": count // 16} if count >= 32 else {"z_lo": 1, "x": 1, "y": count}
    dims |= {"z_hi": 2, "core": 2}
    total = count * 4
    scale = 1.0 / math.sqrt(total * CELLS)
    slab = lax.axis_index("slab")
    core = slab % 2
    feats = features[0]

    label = labels.reshape(CELLS, 1)
    weighting = jnp.where(label == 0, 0.6, jnp.where(label == 1, 2.4, 1.5)).astype(F32)
    weighted = (cotangent.reshape(CELLS, WIDTH).astype(F32) * weighting).astype(BF16)

    row = jnp.where(core == 0, feats[ROWS - 1], feats[0])
    far_row = jnp.where(core == 0, feats[0], feats[ROWS - 1])
    packed = far_row.reshape(COLS, CHANNELS // BLOCK, BLOCK).transpose(1, 0, 2)
    packed = packed.reshape(CHANNELS // BLOCK * COLS, BLOCK)
    packed = jnp.pad(packed, ((0, CELLS - packed.shape[0]), (0, 0)))
    outer = (slab == 0) | (slab == 3)
    message = jnp.where(outer, weighted, packed)
    mirrored = [(d, d - d % 4 + 3 - d % 4) for d in range(total)]
    partner = lax.ppermute(message, AXES, mirrored)
    near = lax.ppermute(row, AXES, [(d, d ^ 1) for d in range(total)])

    payload, own, far = slab_work(
        slab[None].astype(jnp.int32),
        feats,
        near,
        partner,
        weighted,
        first_kernel,
        holed_kernel,
        point_weight,
    )
    arrived = lax.ppermute(far, AXES, [pair for pair in mirrored if pair[0] % 4 in (0, 3)])

    cores = device_groups(dims, "core")
    plane = device_groups(dims, "x", "z_hi", "z_lo")
    ring = device_groups(dims, "y")
    units = payload.reshape(-1, 8, LANES)
    units = scattered(units, cores).astype(BF16)
    units = scattered(units, plane).astype(BF16)
    parts = gathered(units, ring)
    units = (jnp.sum(parts.astype(F32), axis=0) * scale).astype(BF16)
    units = gathered(units, plane).reshape(-1, 8, LANES)
    result = gathered(units, cores).reshape(PAYLOAD_ROWS, LANES)

    branch_out = (own + arrived.astype(F32)).astype(BF16).reshape(1, ROWS, COLS, WIDTH)
    point_grad = jnp.concatenate([result[:CHANNELS], result[CHANNELS : 2 * CHANNELS]], axis=1)
    grads = result[2 * CHANNELS :].reshape(CHANNELS // LANES, GRAD_ROWS, LANES)[:, :18]
    grads = grads.transpose(1, 0, 2).astype(F32).reshape(2, 3, 3, CHANNELS)
    return (branch_out, point_grad, grads[0], grads[1])


def solution(mesh):
    in_specs = (
        P("dp", "slab", None, None),
        P("dp", "slab", None),
        P("dp", "slab", None, None),
        P(),
        P(),
        P(),
    )
    out_specs = (P("dp", "slab", None, None), P(), P(), P())
    return jax.shard_map(
        per_device, mesh=mesh, in_specs=in_specs, out_specs=out_specs, check_vma=False
    )
```

time: 425 us -> 133 us (0.31)
  waiting for transfers between devices: 314 us -> 15.6 us
  blocking collectives: 0 us -> 64.9 us
  other arithmetic: 61.2 us -> 5.54 us
  Pallas kernels: 0 us -> 19 us
  between operations: 14.2 us -> 0.83 us
  matrix products: 5.93 us -> 0 us
    psum x1 -> x0, waiting for transfers between devices: 308 us -> none  [per_device(): lax.psum((point_part, first_part, holed_portion), ('dp', 'slab'))]
    all_to_all x0 -> x4, blocking collectives: none -> 64.9 us  [exchange(): lax.all_to_all(parts, AXES, 0, 0, axis_index_groups=groups, tiled=True)]
    convert_element_type x10 -> x3, other arithmetic: 37.6 us -> 0.76 us  [the longest x1 0.74 us: per_device(): (own + arrived.astype(F32)).astype(BF16).reshape(1, ROWS, COLS, WIDTH)]
    reduce_sum x2 -> x3, other arithmetic: 21.2 us -> 0.71 us  [the longest x2 0.68 us: scattered(): return jnp.sum(parts.astype(F32), axis=0)]
    pallas_call x0 -> x1, Pallas kernels: none -> 19 us  [slab_work(): pl.pallas_call(body, grid_spec=pltpu.PrefetchScalarGridSpec(num_scalar_pr...]
    all_to_all x0 -> x1, waiting for transfers between devices: none -> 11.8 us  [exchange(): lax.all_to_all(parts, AXES, 0, 0, axis_index_groups=groups, tiled=True)]
    ppermute x6 -> x3, starting transfers between devices: 26.1 us -> 14.6 us  [the longest x1 12 us: per_device(): partner = lax.ppermute(message, AXES, mirrored)]
    all_to_all x0 -> x1, starting transfers between devices: none -> 7.9 us  [exchange(): lax.all_to_all(parts, AXES, 0, 0, axis_index_groups=groups, tiled=True)]
  transfers between devices with their start and end apart: 7 -> 4, of which waited for: 2 -> 3; matrix products, arithmetic and copies ran while one was open for 11% -> 1% of each run, Pallas kernels for 0% -> 0%
where the time goes in v1:
time: 133 us; the launch traced here: 132 us
  blocking collectives  64.9 us (49%)
  starting transfers between devices  22.5 us (17%)
  Pallas kernels  19 us (14%)
  waiting for transfers between devices  15.6 us (12%)
  other arithmetic  5.54 us (4%)
  local copies, waits for them, and re-layouts  3.81 us (3%)
    all_to_all x4, blocking collectives, exchange(): lax.all_to_all(parts, AXES, 0, 0, axis_index_groups=groups, tiled=True)  64.9 us
    pallas_call x1, Pallas kernels, slab_work(): pl.pallas_call(body, grid_spec=pltpu.PrefetchScalarGridSpec(num_scalar_pr...  19 us
    ppermute x1, starting transfers between devices, per_device(): partner = lax.ppermute(message, AXES, mirrored)  12 us
    all_to_all x1, waiting for transfers between devices, exchange(): lax.all_to_all(parts, AXES, 0, 0, axis_index_groups=groups, tiled=True)  11.8 us
    all_to_all x1, starting transfers between devices, exchange(): lax.all_to_all(parts, AXES, 0, 0, axis_index_groups=groups, tiled=True)  7.9 us
  transfers between devices with their start and end apart: 4, of which 3 were waited for; matrix products, arithmetic and copies ran while one was open for 1% of the time, Pallas kernels for 0%

profile of v1, /device:TPU:1, one launch (start us, length us, event | category | flops | bytes accessed | tf_op | source)
XLA Modules:
  0.0 132.2 jit_solution(16332146031066189375)
XLA Ops:
  0.6 0.0 copy-start
  0.6 0.0 copy-start.3
  0.7 0.0 copy-start.2
  0.7 0.9 fusion.1
  1.5 0.1 select_n.63
  1.6 1.0 broadcast_select_fusion
  2.7 1.1 pad_select_fusion
  3.8 12.0 %collective-permute-start.1 = (bf16[480,256]{1,0:T(8,128)(2,1)S(1)}, bf16[480,256]{1,0:T(8,128)(2,1)S(1)}, u32[]{:S(2)}, u32[]{:S(2)}) collective-permute-start(bf16[480,256]{1,0:T(8,128)(2,1)S(1)} %get-tuple-element.10), channel_id=1, source_target_pairs={{0,3},{1,2},{2,1},{3,0},{4,7},{5,6},{6,5},{7,4},{8,11},{9,10},{10,... | collective-permute-start | bytes 737288 | tf_op jit(solution)/shard_map/ppermute | solution.py:294
  15.9 1.9 %collective-permute-start = (bf16[40,2048]{1,0:T(8,128)(2,1)S(1)}, bf16[40,2048]{1,0:T(8,128)(2,1)S(1)}, u32[]{:S(2)}, u32[]{:S(2)}) collective-permute-start(bf16[40,2048]{1,0:T(8,128)(2,1)S(1)} %get-tuple-element.13), channel_id=1, source_target_pairs={{0,1},{1,0},{2,3},{3,2},{4,5},{5,4},{6,7},{7,6},{8,9},{9,8},{10,11... | collective-permute-start | bytes 491528 | tf_op jit(solution)/shard_map/ppermute | solution.py:295
  17.8 1.4 %collective-permute-done.near_ref = bf16[40,2048]{1,0:T(8,128)(2,1)S(1)} collective-permute-done((bf16[40,2048]{1,0:T(8,128)(2,1)S(1)}, bf16[40,2048]{1,0:T(8,128)(2,1)S(1)}, u32[]{:S(2)}, u32[]{:S(2)}) %collective-permute-start) | collective-permute-done | bytes 163872 | tf_op jit(solution)/shard_map/ppermute | solution.py:295
  19.2 2.5 %collective-permute-done.1.far_ref.partner_ref = bf16[480,256]{1,0:T(8,128)(2,1)S(1)} collective-permute-done((bf16[480,256]{1,0:T(8,128)(2,1)S(1)}, bf16[480,256]{1,0:T(8,128)(2,1)S(1)}, u32[]{:S(2)}, u32[]{:S(2)}) %collective-permute-start.1) | collective-permute-done | bytes 245792 | tf_op jit(solution)/shard_map/ppermute | solution.py:294
  21.6 0.0 copy-done
  21.6 0.0 copy-done.3
  21.6 0.0 copy-done.2
  21.6 0.0 copy-start.1
  21.6 1.2 copy-done.1
  22.9 19.0 %shard_map.93 = (bf16[4608,128]{1,0:T(8,128)(2,1)S(1)}, f32[480,256]{1,0:T(8,128)S(1)}, bf16[480,256]{1,0:T(8,128)(2,1)S(1)}) custom-call(s32[1]{0:T(128)} %bitcast.slab_ref, bf16[12,40,2048]{2,1,0:T(8,128)(2,1)S(1)} %bitcast.24, bf16[40,2048]{1,0:T(8,128)(2,1)S(1)} %collective-permute-done.near_ref, ...), custom_call_target="tpu_custom_call" | custom-call | flops 3019898880 | bytes 6291456 | tf_op jit(solution)/shard_map/pallas_call | solution.py:229
  41.9 5.9 %all_to_all.25 = bf16[2,288,8,128]{3,2,1,0:T(8,128)(2,1)S(1)} all-to-all(bf16[2,288,8,128]{3,2,1,0:T(8,128)(2,1)S(1)} %bitcast.23), channel_id=1, replica_groups={{0,1},{2,3},{4,5},{6,7},{8,9},{10,11},{12,13},{14,15},{16,17},{18,19},{..., dimensions={0} | all-to-all | bytes 2359296 | tf_op jit(solution)/shard_map/all_to_all | solution.py:44
  47.8 0.6 reduce_sum.33
  48.4 29.6 %all_to_all.26 = bf16[32,9,8,128]{3,2,1,0:T(8,128)(2,1)S(1)} all-to-all(bf16[32,9,8,128]{3,2,1,0:T(8,128)(2,1)S(1)} %bitcast.28), channel_id=1, replica_groups={{0,128,256,384,2,130,258,386,32,160,288,416,34,162,290,418,64,192,320,4..., dimensions={0} | all-to-all | bytes 1179648 | tf_op jit(solution)/shard_map/all_to_all | solution.py:44
  78.0 0.1 reduce_sum.34
  78.2 14.7 %all_to_all.27 = bf16[8,9,8,128]{3,2,1,0:T(8,128)(2,1)S(1)} all-to-all(bf16[8,9,8,128]{3,2,1,0:T(8,128)(2,1)S(1)} %broadcast_in_dim.38), channel_id=1, replica_groups={{0,4,8,12,16,20,24,28},{1,5,9,13,17,21,25,29},{2,6,10,14,18,22,26,30},{..., dimensions={0} | all-to-all | bytes 294912 | tf_op jit(solution)/shard_map/all_to_all | solution.py:44
  92.9 0.9 broadcast_in_dim.39
  93.8 7.9 %all-to-all-start.3 = ((bf16[32,9,8,128]{3,2,1,0:T(8,128)(2,1)}), bf16[32,9,8,128]{3,2,1,0:T(8,128)(2,1)S(1)}, u32[]{:S(2)}, u32[]{:S(2)}) async-start(bf16[32,9,8,128]{3,2,1,0:T(8,128)(2,1)} %broadcast_in_dim.39), calls=%async_computation.3 | async-start | bytes 1179648 | tf_op jit(solution)/shard_map/all_to_all | solution.py:44
  101.7 0.7 collective-permute-start.2
  102.4 0.0 collective-permute-done.2
  102.4 0.7 add_convert_fusion
  103.2 11.8 %all-to-all-done.3 = bf16[32,9,8,128]{3,2,1,0:T(8,128)(2,1)S(1)} async-done(((bf16[32,9,8,128]{3,2,1,0:T(8,128)(2,1)}), bf16[32,9,8,128]{3,2,1,0:T(8,128)(2,1)S(1)}, u32[]{:S(2)}, u32[]{:S(2)}) %all-to-all-start.3) | async-done | bytes 589856 | tf_op jit(solution)/shard_map/all_to_all | solution.py:44
  114.9 0.1 broadcast_in_dim.41
  115.0 14.6 %all_to_all.28 = bf16[2,288,8,128]{3,2,1,0:T(8,128)(2,1)S(1)} all-to-all(bf16[2,288,8,128]{3,2,1,0:T(8,128)(2,1)S(1)} %broadcast_in_dim.41), channel_id=1, replica_groups={{0,1},{2,3},{4,5},{6,7},{8,9},{10,11},{12,13},{14,15},{16,17},{18,19},{..., dimensions={0} | all-to-all | bytes 2359296 | tf_op jit(solution)/shard_map/all_to_all | solution.py:44
  129.7 0.1 fusion.3
  129.8 0.7 squeeze.15
  130.5 0.7 squeeze.14
  131.1 1.1 pad_maximum_fusion
  (9 shorter events, 0.2 us)
Async XLA Ops:
  0.6 21.0 %copy-start = (bf16[1,12,40,2048]{3,2,1,0:T(8,128)(2,1)S(1)}, bf16[1,12,40,2048]{3,2,1,0:T(8,128)(2,1)}, u32[]{:S(2)}) copy-start(bf16[1,12,40,2048]{3,2,1,0:T(8,128)(2,1)} %param.6) | copy-start | bytes 5898244
  0.6 21.0 %copy-start.3 = (f32[3,3,2048]{2,1,0:T(4,128)S(1)}, f32[3,3,2048]{2,1,0:T(4,128)}, u32[]{:S(2)}) copy-start(f32[3,3,2048]{2,1,0:T(4,128)} %holed_k_ref.1) | copy-start | bytes 221188
  0.7 21.0 %copy-start.2 = (f32[3,3,2048]{2,1,0:T(4,128)S(1)}, f32[3,3,2048]{2,1,0:T(4,128)}, u32[]{:S(2)}) copy-start(f32[3,3,2048]{2,1,0:T(4,128)} %first_k_ref.1) | copy-start | bytes 221188
  3.8 17.8 %collective-permute-start.1 = (bf16[480,256]{1,0:T(8,128)(2,1)S(1)}, bf16[480,256]{1,0:T(8,128)(2,1)S(1)}, u32[]{:S(2)}, u32[]{:S(2)}) collective-permute-start(bf16[480,256]{1,0:T(8,128)(2,1)S(1)} %get-tuple-element.10), channel_id=1, source_target_pairs={{0,3},{1,2},{2,1},{3,0},{4,7},{5,6},{6,5},{7,4},{8,11},{9,10},{10,... | collective-permute-start | bytes 737288 | tf_op jit(solution)/shard_map/ppermute | solution.py:294
  15.9 3.3 %collective-permute-start = (bf16[40,2048]{1,0:T(8,128)(2,1)S(1)}, bf16[40,2048]{1,0:T(8,128)(2,1)S(1)}, u32[]{:S(2)}, u32[]{:S(2)}) collective-permute-start(bf16[40,2048]{1,0:T(8,128)(2,1)S(1)} %get-tuple-element.13), channel_id=1, source_target_pairs={{0,1},{1,0},{2,3},{3,2},{4,5},{5,4},{6,7},{7,6},{8,9},{9,8},{10,11... | collective-permute-start | bytes 491528 | tf_op jit(solution)/shard_map/ppermute | solution.py:295
  21.6 1.2 copy-start.1
  93.8 21.1 %all-to-all-start.3 = ((bf16[32,9,8,128]{3,2,1,0:T(8,128)(2,1)}), bf16[32,9,8,128]{3,2,1,0:T(8,128)(2,1)S(1)}, u32[]{:S(2)}, u32[]{:S(2)}) async-start(bf16[32,9,8,128]{3,2,1,0:T(8,128)(2,1)} %broadcast_in_dim.39), calls=%async_computation.3 | async-start | bytes 1179648 | tf_op jit(solution)/shard_map/all_to_all | solution.py:44
  101.7 0.7 collective-permute-start.2

commit v2 on v1

v2 whole, which is shorter than its diff:
```python
import itertools
import math

import jax
import jax.numpy as jnp
from jax import lax
from jax.experimental import pallas as pl
from jax.experimental.pallas import tpu as pltpu
from jax.sharding import PartitionSpec as P

AXES = ("dp", "slab")
STEP = 36
ROWS = 12
COLS = 40
CELLS = ROWS * COLS
EDGE = COLS - STEP
CHANNELS = 2048
WIDTH = 256
BLOCK = 512
PACKED = 256
LANES = 128
GRAD_ROWS = 32
PAYLOAD_ROWS = 2 * CHANNELS + CHANNELS // LANES * GRAD_ROWS
F32 = jnp.float32
BF16 = jnp.bfloat16


def device_groups(dims, *names):
    strides, stride = {}, 1
    for name in reversed(dims):
        strides[name] = stride
        stride *= dims[name]

    def places(chosen):
        return [
            sum(i * strides[n] for n, i in zip(chosen, spot))
            for spot in itertools.product(*(range(dims[n]) for n in chosen))
        ]

    inside = places(names)
    return [[base + i for i in inside] for base in places([n for n in dims if n not in names])]


def exchange(parts, groups):
    return lax.all_to_all(parts, AXES, 0, 0, axis_index_groups=groups, tiled=True)


def scattered(units, groups):
    count = len(groups[0])
    parts = exchange(units.reshape(count, units.shape[0] // count, 8, LANES), groups)
    return jnp.sum(parts.astype(F32), axis=0)


def gathered(units, groups):
    count = len(groups[0])
    return exchange(jnp.broadcast_to(units[None], (count, *units.shape)), groups)


def widened(xs, x_ref, near, far, slab):
    core = lax.rem(slab, 2)
    one = jnp.where(core == 1, 1.0, 0.0)
    xs[pl.ds(0, COLS), :] = near * one + far * jnp.where(slab == 2, 1.0, 0.0)
    xs[pl.ds((ROWS + 1) * COLS, COLS), :] = near * (1.0 - one) + far * jnp.where(slab == 1, 1.0, 0.0)

    for r in range(ROWS):
        xs[pl.ds((r + 1) * COLS, COLS), :] = x_ref[r].astype(F32)


def from_left(v):
    sub = lax.broadcasted_iota(jnp.int32, (8, v.shape[1]), 0)
    moved = pltpu.roll(v, 1, 0)
    return jnp.concatenate([jnp.where(sub == 0, 0.0, moved[:8]), moved[8:]], 0)


def from_right(v):
    sub = lax.broadcasted_iota(jnp.int32, (8, v.shape[1]), 0)
    moved = pltpu.roll(v, COLS - 1, 0)
    return jnp.concatenate([moved[: COLS - 8], jnp.where(sub == 7, 0.0, moved[COLS - 8 :])], 0)


def fold(v):
    parts = [v[8 * i : 8 * i + 8] for i in range(COLS // 8)]
    while len(parts) > 1:
        parts = [a + b for a, b in zip(parts[::2], parts[1::2])] + (
            parts[-1:] if len(parts) % 2 else []
        )
    return parts[0]


def conv_row(fk, x):
    side = [fk[0][j] * x[0] + fk[1][j] * x[1] + fk[2][j] * x[2] for j in range(3)]
    return side[1] + from_left(side[0]) + from_right(side[2])


def ends(v):
    low = lax.broadcasted_iota(jnp.int32, (8, LANES), 0) < EDGE
    high_end = jnp.where(low, pltpu.roll(v[COLS - 8 :], 4, 0), 0.0)
    low_end = jnp.where(low, 0.0, pltpu.roll(v[:8], 4, 0))
    return high_end, low_end


def spread(k, v, v_ends):
    c = k[1] * v
    return jnp.concatenate(
        [c[:8] + k[2] * v_ends[0], c[8 : COLS - 8], c[COLS - 8 :] + k[0] * v_ends[1]], 0
    )


def taps(ref, lanes):
    return [[ref[i, j : j + 1, lanes] for j in range(3)] for i in range(3)]


def far_taps(hk, slab):
    up = jnp.where(slab == 0, 1.0, 0.0)
    down = jnp.where(slab == 3, 1.0, 0.0)
    return [hk[0][j] * up + hk[2][j] * down for j in range(3)]


def first_body(
    slab_ref, x_ref, near_ref, first_k_ref, holed_k_ref, point_ref, f_ref, far_out_ref, xs, a_far, far_acc
):
    step = pl.program_id(0)
    slab = slab_ref[0]

    @pl.when(step == 0)
    def _():
        far_acc[...] = jnp.zeros_like(far_acc)

    widened(xs, x_ref, near_ref[...].astype(F32), jnp.zeros((COLS, BLOCK), F32), slab)
    for chunk in range(BLOCK // LANES):
        lanes = pl.ds(chunk * LANES, LANES)
        fk = taps(first_k_ref, lanes)
        kf = far_taps(taps(holed_k_ref, lanes), slab)

        for p in range(ROWS // 2):
            base = p * 2 * COLS
            x = [xs[pl.ds(base + i * COLS, COLS), lanes] for i in range(4)]
            far_rows = []
            for r in range(2):
                f16 = conv_row(fk, x[r : r + 3]).astype(BF16)
                f_ref[2 * p + r, :, lanes] = f16
                f = f16.astype(F32)
                far_rows.append(spread(kf, f, ends(f)))
            a_far[pl.ds(base, 2 * COLS), lanes] = jnp.concatenate(far_rows, 0).astype(BF16)

    far_acc[...] += jnp.dot(a_far[...], point_ref[...], preferred_element_type=F32)

    @pl.when(step == pl.num_programs(0) - 1)
    def _():
        far_out_ref[...] = far_acc[...].astype(BF16)


def second_body(
    slab_ref,
    x_ref,
    near_ref,
    far_ref,
    weighted_ref,
    partner_ref,
    f_ref,
    first_k_ref,
    holed_k_ref,
    point_ref,
    payload_ref,
    own_out_ref,
    xs,
    wfar,
    b_own,
    b_far,
    a_own,
    a_far,
    f_edge,
    own_acc,
):
    step = pl.program_id(0)
    slab = slab_ref[0]
    edge = jnp.where(lax.rem(slab, 2) == 0, 0, ROWS - 1)
    up = jnp.where(slab == 0, 1.0, 0.0)
    down = jnp.where(slab == 3, 1.0, 0.0)

    @pl.when(step == 0)
    def _():
        wfar[...] = (partner_ref[...].astype(F32) * (up + down)).astype(BF16)
        own_acc[...] = jnp.zeros_like(own_acc)

    far = far_ref[...].astype(F32)
    far = jnp.concatenate([far[i * COLS : (i + 1) * COLS] for i in range(BLOCK // PACKED)], 1)
    widened(xs, x_ref, near_ref[...].astype(F32), far, slab)

    weights = point_ref[...]
    nt = (((1,), (1,)), ((), ()))
    tn = (((0,), (0,)), ((), ()))
    for given, back in ((weighted_ref, b_own), (wfar, b_far)):
        product = lax.dot_general(given[...], weights, nt, preferred_element_type=F32)
        back[...] = product.astype(BF16).astype(F32)

    for chunk in range(BLOCK // LANES):
        lanes = pl.ds(chunk * LANES, LANES)
        fk = taps(first_k_ref, lanes)
        hk = taps(holed_k_ref, lanes)
        mk = hk[1]
        kf = far_taps(hk, slab)
        x = [xs[pl.ds(pl.multiple_of((edge + i) * COLS, 8), COLS), lanes] for i in range(3)]
        f_edge[...] = conv_row(fk, x).astype(BF16).astype(F32)

        zero = jnp.zeros((8, LANES), F32)
        first_acc, own_g, far_g = [zero] * 9, [zero] * 3, [zero] * 3
        for p in range(ROWS // 2):
            base = p * 2 * COLS
            own_rows, far_rows = [], []
            for r in range(2):
                here = pl.ds(base + r * COLS, COLS)
                f = f_ref[2 * p + r, :, lanes].astype(F32)
                if 2 * p + r in (0, ROWS - 1):
                    f = jnp.where(2 * p + r == edge, f_edge[...], f)
                bo, bf = b_own[here, lanes], b_far[here, lanes]
                f_ends = ends(f)
                own_rows.append(spread(mk, f, f_ends))
                far_rows.append(spread(kf, f, f_ends))
                for sums, b in ((own_g, bo), (far_g, bf)):
                    sums[0] += f_ends[1] * b[COLS - 8 :]
                    sums[1] += fold(f * b)
                    sums[2] += f_ends[0] * b[:8]
                bo_ends, bf_ends = ends(bo), ends(bf)
                g = spread(mk[::-1], bo, bo_ends) + spread(kf[::-1], bf, bf_ends)
                g = g.astype(BF16).astype(F32)
                shifted = [from_right(g), g, from_left(g)]
                for i in range(3):
                    x = xs[pl.ds(base + (r + i) * COLS, COLS), lanes]
                    for j in range(3):
                        first_acc[3 * i + j] += fold(x * shifted[j])
            there = pl.ds(base, 2 * COLS)
            a_own[there, lanes] = jnp.concatenate(own_rows, 0).astype(BF16)
            a_far[there, lanes] = jnp.concatenate(far_rows, 0).astype(BF16)

        def line(v):
            return jnp.sum(v, axis=0, keepdims=True)

        far_lines = [line(v) for v in far_g]
        lines = [line(v) for v in first_acc]
        lines += [v * up for v in far_lines]
        lines += [line(v) for v in own_g]
        lines += [v * down for v in far_lines]
        lines.append(jnp.zeros((GRAD_ROWS - len(lines), LANES), F32))
        at = 2 * CHANNELS + (step * (BLOCK // LANES) + chunk) * GRAD_ROWS
        payload_ref[pl.ds(pl.multiple_of(at, GRAD_ROWS), GRAD_ROWS), :] = jnp.concatenate(
            lines, 0
        ).astype(BF16)

    own_acc[...] += jnp.dot(a_own[...], weights, preferred_element_type=F32)
    part = lax.dot_general(a_own[...], weighted_ref[...], tn, preferred_element_type=F32)
    part += lax.dot_general(a_far[...], wfar[...], tn, preferred_element_type=F32)
    for half in range(WIDTH // LANES):
        at = pl.multiple_of(half * CHANNELS + step * BLOCK, BLOCK)
        payload_ref[pl.ds(at, BLOCK), :] = part[:, half * LANES : (half + 1) * LANES].astype(BF16)

    @pl.when(step == pl.num_programs(0) - 1)
    def _():
        own_out_ref[...] = own_acc[...]


def whole(shape):
    return pl.BlockSpec(shape, lambda k, s: (0,) * len(shape))


def kernel_call(body, in_specs, out_specs, out_shape, scratch_shapes, flops):
    return pl.pallas_call(
        body,
        grid_spec=pltpu.PrefetchScalarGridSpec(
            num_scalar_prefetch=1,
            grid=(CHANNELS // BLOCK,),
            in_specs=in_specs,
            out_specs=out_specs,
            scratch_shapes=scratch_shapes,
        ),
        out_shape=out_shape,
        compiler_params=pltpu.CompilerParams(vmem_limit_bytes=40 * 2**20),
        cost_estimate=pl.CostEstimate(flops=flops, bytes_accessed=8 * 2**20, transcendentals=0),
    )


SLAB_SPEC = pl.BlockSpec((ROWS, COLS, BLOCK), lambda k, s: (0, 0, k))
LINE_SPEC = pl.BlockSpec((COLS, BLOCK), lambda k, s: (0, k))
TAPS_SPEC = pl.BlockSpec((3, 3, BLOCK), lambda k, s: (0, 0, k))
POINT_SPEC = pl.BlockSpec((BLOCK, WIDTH), lambda k, s: (k, 0))
CELLS_SPEC = whole((CELLS, WIDTH))


def first_work(slab, features, near, first_kernel, holed_kernel, point_weight):
    return kernel_call(
        first_body,
        [SLAB_SPEC, LINE_SPEC, TAPS_SPEC, TAPS_SPEC, POINT_SPEC],
        [SLAB_SPEC, CELLS_SPEC],
        [
            jax.ShapeDtypeStruct((ROWS, COLS, CHANNELS), BF16),
            jax.ShapeDtypeStruct((CELLS, WIDTH), BF16),
        ],
        [
            pltpu.VMEM(((ROWS + 2) * COLS, BLOCK), F32),
            pltpu.VMEM((CELLS, BLOCK), BF16),
            pltpu.VMEM((CELLS, WIDTH), F32),
        ],
        2 * 2 * CELLS * CHANNELS * WIDTH,
    )(slab, features, near, first_kernel, holed_kernel, point_weight)


def second_work(slab, features, near, partner, weighted, first, first_kernel, holed_kernel, point_weight):
    packs = BLOCK // PACKED
    return kernel_call(
        second_body,
        [
            SLAB_SPEC,
            LINE_SPEC,
            pl.BlockSpec((packs * COLS, PACKED), lambda k, s: (k, 0)),
            CELLS_SPEC,
            CELLS_SPEC,
            SLAB_SPEC,
            TAPS_SPEC,
            TAPS_SPEC,
            POINT_SPEC,
        ],
        [whole((PAYLOAD_ROWS, LANES)), CELLS_SPEC],
        [
            jax.ShapeDtypeStruct((PAYLOAD_ROWS, LANES), BF16),
            jax.ShapeDtypeStruct((CELLS, WIDTH), F32),
        ],
        [
            pltpu.VMEM(((ROWS + 2) * COLS, BLOCK), F32),
            pltpu.VMEM((CELLS, WIDTH), BF16),
            pltpu.VMEM((CELLS, BLOCK), F32),
            pltpu.VMEM((CELLS, BLOCK), F32),
            pltpu.VMEM((CELLS, BLOCK), BF16),
            pltpu.VMEM((CELLS, BLOCK), BF16),
            pltpu.VMEM((COLS, LANES), F32),
            pltpu.VMEM((CELLS, WIDTH), F32),
        ],
        10 * 2 * CELLS * CHANNELS * WIDTH,
    )(
        slab,
        features,
        near,
        partner,
        weighted,
        partner,
        first,
        first_kernel,
        holed_kernel,
        point_weight,
    )


def prepare_body(slab_ref, label_ref, cot_ref, near_ref, far_ref, row_ref, message_ref, weighted_ref):
    slab = slab_ref[0]
    outer = jnp.logical_or(slab == 0, slab == 3)
    row_ref[...] = near_ref[0]
    diagonal = lax.broadcasted_iota(jnp.int32, (COLS, COLS), 0) == lax.broadcasted_iota(
        jnp.int32, (COLS, COLS), 1
    )
    for p in range(ROWS // 2):
        pair = pl.ds(2 * COLS * p, 2 * COLS)
        columns = []
        for r in range(2 * p, 2 * p + 2):
            label = label_ref[r]
            weight = jnp.where(label == 0, 0.6, jnp.where(label == 1, 2.4, 1.5)).astype(F32)
            spot = jnp.where(diagonal, jnp.broadcast_to(weight, (COLS, COLS)), 0.0)
            columns.append(jnp.sum(spot, axis=1, keepdims=True))
        scaled = (cot_ref[pair, :].astype(F32) * jnp.concatenate(columns, 0)).astype(BF16)
        weighted_ref[pair, :] = scaled

    @pl.when(outer)
    def _():
        message_ref[...] = weighted_ref[...]

    @pl.when(jnp.logical_not(outer))
    def _():
        packs = CHANNELS // PACKED
        for q in range(0, packs, 2):
            two = [far_ref[0, :, (q + i) * PACKED : (q + i + 1) * PACKED].astype(F32) for i in range(2)]
            message_ref[pl.ds(q * COLS, 2 * COLS), :] = jnp.concatenate(two, 0).astype(BF16)
        rest = CELLS - packs * COLS
        message_ref[pl.ds(packs * COLS, rest), :] = jnp.zeros((rest, WIDTH), BF16)


def prepare(slab, features, labels, cotangent):
    def edge_row(far):
        last = lambda s: (ROWS - 1) * lax.rem(s[0] + 1 - far, 2)
        return pl.BlockSpec((1, COLS, CHANNELS), lambda k, s: (last(s), 0, 0))

    cells = jax.ShapeDtypeStruct((CELLS, WIDTH), BF16)
    return pl.pallas_call(
        prepare_body,
        grid_spec=pltpu.PrefetchScalarGridSpec(
            num_scalar_prefetch=1,
            grid=(1,),
            in_specs=[whole((ROWS, 1, COLS)), CELLS_SPEC, edge_row(0), edge_row(1)],
            out_specs=[whole((COLS, CHANNELS)), CELLS_SPEC, CELLS_SPEC],
        ),
        out_shape=[jax.ShapeDtypeStruct((COLS, CHANNELS), BF16), cells, cells],
        compiler_params=pltpu.CompilerParams(vmem_limit_bytes=56 * 2**20),
    )(slab, labels, cotangent, features, features)


def finish_body(left_ref, right_ref, lines_ref, point_ref, first_ref, atrous_ref):
    point_ref[:, :LANES] = left_ref[...]
    point_ref[:, LANES:] = right_ref[...]

    @pl.when(pl.program_id(0) == 0)
    def _():
        for q in range(CHANNELS // LANES):
            lanes = pl.ds(q * LANES, LANES)
            lines = lines_ref[pl.ds(q * GRAD_ROWS, GRAD_ROWS), :].astype(F32)
            for i in range(3):
                first_ref[i, :, lanes] = lines[3 * i : 3 * i + 3]
                atrous_ref[i, :, lanes] = lines[9 + 3 * i : 12 + 3 * i]


def finish(result):
    steps = 4
    block = CHANNELS // steps
    taps_shape = jax.ShapeDtypeStruct((3, 3, CHANNELS), F32)
    taps_spec = pl.BlockSpec((3, 3, CHANNELS), lambda k: (0, 0, 0))
    return pl.pallas_call(
        finish_body,
        grid=(steps,),
        in_specs=[
            pl.BlockSpec((block, LANES), lambda k: (k, 0)),
            pl.BlockSpec((block, LANES), lambda k: (k + steps, 0)),
            pl.BlockSpec((block, LANES), lambda k: (2 * steps, 0)),
        ],
        out_specs=[pl.BlockSpec((block, WIDTH), lambda k: (k, 0)), taps_spec, taps_spec],
        out_shape=[jax.ShapeDtypeStruct((CHANNELS, WIDTH), BF16), taps_shape, taps_shape],
        compiler_params=pltpu.CompilerParams(vmem_limit_bytes=16 * 2**20),
    )(result, result, result)


def per_device(features, labels, cotangent, first_kernel, holed_kernel, point_weight):
    count = lax.axis_size("dp")
    wide = count >= 32
    dims = {"z_mid": 2 if wide else 1, "z_low": 2 if wide else 1, "x": 4 if wide else 1}
    dims |= {"y_high": count // 32 if wide else 1, "y_low": 2, "z_top": 2, "core": 2}
    total = count * 4
    scale = 1.0 / math.sqrt(total * CELLS)
    slab = lax.axis_index("slab")
    where = slab[None].astype(jnp.int32)
    feats = features[0]
    row, message, weighted = prepare(
        where, feats, labels.reshape(ROWS, 1, COLS), cotangent.reshape(CELLS, WIDTH)
    )
    mirrored = [(d, d - d % 4 + 3 - d % 4) for d in range(total)]
    partner = lax.ppermute(message, AXES, mirrored)
    near = lax.ppermute(row, AXES, [(d, d ^ 1) for d in range(total)])

    first, far = first_work(where, feats, near, first_kernel, holed_kernel, point_weight)
    arrived = lax.ppermute(far, AXES, [pair for pair in mirrored if pair[0] % 4 in (0, 3)])

    payload, own = second_work(
        where, feats, near, partner, weighted, first, first_kernel, holed_kernel, point_weight
    )

    cores = device_groups(dims, "core")
    block = device_groups(dims, "z_low", "x", "y_low")
    z_ring = device_groups(dims, "z_top", "z_mid")
    y_ring = device_groups(dims, "y_high")
    units = payload.reshape(-1, 8, LANES)
    units = scattered(units, cores).astype(BF16)
    units, arrived = lax.optimization_barrier((units, arrived))
    units = scattered(units, block).astype(BF16)
    units = jnp.sum(gathered(units, z_ring).astype(F32), axis=0).astype(BF16)
    units = (jnp.sum(gathered(units, y_ring).astype(F32), axis=0) * scale).astype(BF16)
    units = gathered(units, block).reshape(-1, 8, LANES)
    result = gathered(units, cores).reshape(PAYLOAD_ROWS, LANES)

    branch_out = (own + arrived.astype(F32)).astype(BF16).reshape(1, ROWS, COLS, WIDTH)
    point_grad, first_grad, atrous_grad = finish(result)
    return (branch_out, point_grad, first_grad, atrous_grad)


def solution(mesh):
    in_specs = (
        P("dp", "slab", None, None),
        P("dp", "slab", None),
        P("dp", "slab", None, None),
        P(),
        P(),
        P(),
    )
    out_specs = (P("dp", "slab", None, None), P(), P(), P())
    return jax.shard_map(
        per_device, mesh=mesh, in_specs=in_specs, out_specs=out_specs, check_vma=False
    )
```

time: 133 us -> 113 us (0.85)
  blocking collectives: 64.9 us -> 60 us
  waiting for transfers between devices: 15.6 us -> 11.3 us
  starting transfers between devices: 22.5 us -> 18.3 us
  other arithmetic: 5.54 us -> 1.47 us
  local copies, waits for them, and re-layouts: 3.81 us -> 1.03 us
    ppermute x1, starting transfers between devices: 1.92 us -> 8.77 us  [per_device(): near = lax.ppermute(row, AXES, [(d, d ^ 1) for d in range(total)])]
    ppermute x1, starting transfers between devices: 12 us -> 5.3 us  [per_device(): partner = lax.ppermute(message, AXES, mirrored)]
    all_to_all x4 -> x5, blocking collectives: 64.9 us -> 60 us  [exchange(): lax.all_to_all(parts, AXES, 0, 0, axis_index_groups=groups, tiled=True)]
    all_to_all x1, waiting for transfers between devices: 11.8 us -> 7.01 us  [exchange(): lax.all_to_all(parts, AXES, 0, 0, axis_index_groups=groups, tiled=True)]
    all_to_all x1, starting transfers between devices: 7.9 us -> 3.58 us  [exchange(): lax.all_to_all(parts, AXES, 0, 0, axis_index_groups=groups, tiled=True)]
    select_n x3 -> x0, other arithmetic: 2.98 us -> none  [the longest x1 1.1 us: per_device(): message = jnp.where(outer, weighted, packed)]
    ppermute x1, waiting for transfers between devices: 2.46 us -> 4.27 us  [per_device(): partner = lax.ppermute(message, AXES, mirrored)]
    ppermute x1, waiting for transfers between devices: 1.36 us -> 0.01 us  [per_device(): near = lax.ppermute(row, AXES, [(d, d ^ 1) for d in range(total)])]
  transfers between devices with their start and end apart: 4 -> 4, of which waited for: 3 -> 2; matrix products, arithmetic and copies ran while one was open for 1% -> 1% of each run, Pallas kernels for 0% -> 14%
where the time goes in v2:
time: 113 us
  blocking collectives  60 us (53%)
  Pallas kernels  19.7 us (17%)
  starting transfers between devices  18.3 us (16%)
  waiting for transfers between devices  11.3 us (10%)
  other arithmetic  1.47 us (1%)
    all_to_all x5, blocking collectives, exchange(): lax.all_to_all(parts, AXES, 0, 0, axis_index_groups=groups, tiled=True)  60 us
    pallas_call x1, Pallas kernels, second_work(): kernel_call(second_body, [SLAB_SPEC, LINE_SPEC, pl.BlockSpec((packs * COL...  10.2 us
    ppermute x1, starting transfers between devices, per_device(): near = lax.ppermute(row, AXES, [(d, d ^ 1) for d in range(total)])  8.77 us
    all_to_all x1, waiting for transfers between devices, exchange(): lax.all_to_all(parts, AXES, 0, 0, axis_index_groups=groups, tiled=True)  7.01 us
    pallas_call x1, Pallas kernels, first_work(): kernel_call(first_body, [SLAB_SPEC, LINE_SPEC, TAPS_SPEC, TAPS_SPEC, POIN...  5.36 us
    ppermute x1, starting transfers between devices, per_device(): partner = lax.ppermute(message, AXES, mirrored)  5.3 us
    ppermute x1, waiting for transfers between devices, per_device(): partner = lax.ppermute(message, AXES, mirrored)  4.27 us
    all_to_all x1, starting transfers between devices, exchange(): lax.all_to_all(parts, AXES, 0, 0, axis_index_groups=groups, tiled=True)  3.58 us
  transfers between devices with their start and end apart: 4, of which 2 were waited for; matrix products, arithmetic and copies ran while one was open for 1% of the time, Pallas kernels for 14%

profile of v2, /device:TPU:1, one launch (start us, length us, event | category | flops | bytes accessed | tf_op | source)
XLA Modules:
  0.0 112.6 jit_solution(14930794033025191594)
XLA Ops:
  0.6 0.0 copy-start
  0.6 0.0 copy-start.1
  0.7 0.0 copy-start.3
  0.7 0.0 copy-start.4
  0.7 2.4 %shard_map.93 = (bf16[40,2048]{1,0:T(8,128)(2,1)}, bf16[480,256]{1,0:T(8,128)(2,1)}, bf16[480,256]{1,0:T(8,128)(2,1)}) custom-call(s32[1]{0:T(128)} %bitcast.slab_ref, s32[12,1,40]{2,1,0:T(1,128)} %bitcast.21, bf16[480,256]{1,0:T(8,128)(2,1)} %bitcast.19, bf16[12,40,2048]{2,1,0:T(8,128)(2,1)} %bitcast.12, bf16[12,40,2048]{2,1,0:T(8,128)(2,1)} %bitcast.13), custom_call_target="tpu_custom_call" | custom-call | tf_op jit(solution)/shard_map/pallas_call | solution.py:390
  3.1 8.8 %collective-permute-start = (bf16[40,2048]{1,0:T(8,128)(2,1)}, bf16[40,2048]{1,0:T(8,128)(2,1)S(1)}, u32[]{:S(2)}, u32[]{:S(2)}) collective-permute-start(bf16[40,2048]{1,0:T(8,128)(2,1)} %get-tuple-element.16), channel_id=1, source_target_pairs={{0,1},{1,0},{2,3},{3,2},{4,5},{5,4},{6,7},{7,6},{8,9},{9,8},{10,11... | collective-permute-start | bytes 491528 | tf_op jit(solution)/shard_map/ppermute | solution.py:451
  11.8 0.0 copy-start.2
  11.9 5.3 %collective-permute-start.1 = (bf16[480,256]{1,0:T(8,128)(2,1)}, bf16[480,256]{1,0:T(8,128)(2,1)S(1)}, u32[]{:S(2)}, u32[]{:S(2)}) collective-permute-start(bf16[480,256]{1,0:T(8,128)(2,1)} %get-tuple-element.17), channel_id=1, source_target_pairs={{0,3},{1,2},{2,1},{3,0},{4,7},{5,6},{6,5},{7,4},{8,11},{9,10},{10,... | collective-permute-start | bytes 737288 | tf_op jit(solution)/shard_map/ppermute | solution.py:450
  17.2 0.0 collective-permute-done.near_ref
  17.2 0.0 copy-done
  17.2 0.0 copy-done.1
  17.2 0.0 copy-done.3
  17.2 0.0 copy-done.4
  17.2 5.4 %shard_map.94 = (bf16[12,40,2048]{2,1,0:T(8,128)(2,1)S(1)}, bf16[480,256]{1,0:T(8,128)(2,1)S(1)}) custom-call(s32[1]{0:T(128)} %bitcast.slab_ref, bf16[12,40,2048]{2,1,0:T(8,128)(2,1)S(1)} %bitcast.14, bf16[40,2048]{1,0:T(8,128)(2,1)S(1)} %collective-permute-done.near_ref, f32[3,3,2048]{2,1,0:T(4,128)S(1)} %copy-done.3, f32[3,3,2048]{2,1,0:T(4,128)S(1)} %copy-done.4, ...), custom_call_target="tpu_custom_call" | custom-call | flops 1006632960 | bytes 8388608 | tf_op jit(solution)/shard_map/pallas_call | solution.py:290
  22.6 0.7 collective-permute-start.2
  23.3 4.3 %collective-permute-done.1.far_ref.partner_ref = bf16[480,256]{1,0:T(8,128)(2,1)S(1)} collective-permute-done((bf16[480,256]{1,0:T(8,128)(2,1)}, bf16[480,256]{1,0:T(8,128)(2,1)S(1)}, u32[]{:S(2)}, u32[]{:S(2)}) %collective-permute-start.1) | collective-permute-done | bytes 245792 | tf_op jit(solution)/shard_map/ppermute | solution.py:450
  27.5 0.0 copy-done.2
  27.5 10.2 %shard_map.95 = (bf16[4608,128]{1,0:T(8,128)(2,1)S(1)}, f32[480,256]{1,0:T(8,128)S(1)}) custom-call(s32[1]{0:T(128)} %bitcast.slab_ref, bf16[12,40,2048]{2,1,0:T(8,128)(2,1)S(1)} %bitcast.15, bf16[40,2048]{1,0:T(8,128)(2,1)S(1)} %collective-permute-done.near_ref, bf16[480,256]{1,0:T(8,128)(2,1)S(1)} %collective-permute-done.1.far_ref.partner_ref, ...), custom_call_target="tpu_custom_call" | custom-call | flops 5033164800 | bytes 8388608 | tf_op jit(solution)/shard_map/pallas_call | solution.py:309
  37.8 4.4 %all_to_all.30 = bf16[2,288,8,128]{3,2,1,0:T(8,128)(2,1)S(1)} all-to-all(bf16[2,288,8,128]{3,2,1,0:T(8,128)(2,1)S(1)} %bitcast.16), channel_id=1, replica_groups={{0,1},{2,3},{4,5},{6,7},{8,9},{10,11},{12,13},{14,15},{16,17},{18,19},{..., dimensions={0} | all-to-all | bytes 2359296 | tf_op jit(solution)/shard_map/all_to_all | solution.py:45
  42.1 0.6 reduce_sum.45
  42.7 0.0 collective-permute-done.2
  42.7 18.4 %all_to_all.31 = bf16[16,18,8,128]{3,2,1,0:T(8,128)(2,1)S(1)} all-to-all(bf16[16,18,8,128]{3,2,1,0:T(8,128)(2,1)S(1)} %bitcast.18), channel_id=1, replica_groups={{0,4,32,36,64,68,96,100,128,132,160,164,192,196,224,228},{1,5,33,37,65,..., dimensions={0} | all-to-all | bytes 1179648 | tf_op jit(solution)/shard_map/all_to_all | solution.py:45
  61.2 0.1 reduce_sum.46
  61.3 13.2 %all_to_all.32 = bf16[4,18,8,128]{3,2,1,0:T(8,128)(2,1)S(1)} all-to-all(bf16[4,18,8,128]{3,2,1,0:T(8,128)(2,1)S(1)} %broadcast_in_dim.13), channel_id=1, replica_groups={{0,256,2,258},{1,257,3,259},{4,260,6,262},{5,261,7,263},{8,264,10,266},..., dimensions={0} | all-to-all | bytes 294912 | tf_op jit(solution)/shard_map/all_to_all | solution.py:45
  74.6 13.7 %all_to_all.33 = bf16[4,18,8,128]{3,2,1,0:T(8,128)(2,1)S(1)} all-to-all(bf16[4,18,8,128]{3,2,1,0:T(8,128)(2,1)S(1)} %broadcast_in_dim.14), channel_id=1, replica_groups={{0,8,16,24},{1,9,17,25},{2,10,18,26},{3,11,19,27},{4,12,20,28},{5,13,21..., dimensions={0} | all-to-all | bytes 294912 | tf_op jit(solution)/shard_map/all_to_all | solution.py:45
  88.3 0.9 broadcast_in_dim.15
  89.2 3.6 %all-to-all-start.4 = ((bf16[16,18,8,128]{3,2,1,0:T(8,128)(2,1)}), bf16[16,18,8,128]{3,2,1,0:T(8,128)(2,1)S(1)}, u32[]{:S(2)}, u32[]{:S(2)}) async-start(bf16[16,18,8,128]{3,2,1,0:T(8,128)(2,1)} %broadcast_in_dim.15), calls=%async_computation.4 | async-start | bytes 1179648 | tf_op jit(solution)/shard_map/all_to_all | solution.py:45
  92.8 0.7 add_convert_fusion
  93.5 7.0 %all-to-all-done.4 = bf16[16,18,8,128]{3,2,1,0:T(8,128)(2,1)S(1)} async-done(((bf16[16,18,8,128]{3,2,1,0:T(8,128)(2,1)}), bf16[16,18,8,128]{3,2,1,0:T(8,128)(2,1)S(1)}, u32[]{:S(2)}, u32[]{:S(2)}) %all-to-all-start.4) | async-done | bytes 589856 | tf_op jit(solution)/shard_map/all_to_all | solution.py:45
  100.5 0.1 broadcast_in_dim.33
  100.6 10.4 %all_to_all.34 = bf16[2,288,8,128]{3,2,1,0:T(8,128)(2,1)S(1)} all-to-all(bf16[2,288,8,128]{3,2,1,0:T(8,128)(2,1)S(1)} %broadcast_in_dim.33), channel_id=1, replica_groups={{0,1},{2,3},{4,5},{6,7},{8,9},{10,11},{12,13},{14,15},{16,17},{18,19},{..., dimensions={0} | all-to-all | bytes 2359296 | tf_op jit(solution)/shard_map/all_to_all | solution.py:45
  110.9 1.7 %shard_map.96 = (bf16[2048,256]{1,0:T(8,128)(2,1)}, f32[3,3,2048]{2,1,0:T(4,128)}, f32[3,3,2048]{2,1,0:T(4,128)}) custom-call(bf16[4608,128]{1,0:T(8,128)(2,1)S(1)} %bitcast.9, bf16[4608,128]{1,0:T(8,128)(2,1)S(1)} %bitcast.10, bf16[4608,128]{1,0:T(8,128)(2,1)S(1)} %bitcast.11), custom_call_target="tpu_custom_call" | custom-call | tf_op jit(solution)/shard_map/pallas_call | solution.py:422
  (5 shorter events, 0.1 us)
Async XLA Ops:
  0.6 16.5 %copy-start = (bf16[1,12,40,2048]{3,2,1,0:T(8,128)(2,1)S(1)}, bf16[1,12,40,2048]{3,2,1,0:T(8,128)(2,1)}, u32[]{:S(2)}) copy-start(bf16[1,12,40,2048]{3,2,1,0:T(8,128)(2,1)} %param.6) | copy-start | bytes 5898244
  0.6 16.5 %copy-start.1 = (bf16[2048,256]{1,0:T(8,128)(2,1)S(1)}, bf16[2048,256]{1,0:T(8,128)(2,1)}, u32[]{:S(2)}) copy-start(bf16[2048,256]{1,0:T(8,128)(2,1)} %point_ref.3) | copy-start | bytes 3145732
  0.7 16.5 %copy-start.3 = (f32[3,3,2048]{2,1,0:T(4,128)S(1)}, f32[3,3,2048]{2,1,0:T(4,128)}, u32[]{:S(2)}) copy-start(f32[3,3,2048]{2,1,0:T(4,128)} %first_k_ref.3) | copy-start | bytes 221188
  0.7 16.5 %copy-start.4 = (f32[3,3,2048]{2,1,0:T(4,128)S(1)}, f32[3,3,2048]{2,1,0:T(4,128)}, u32[]{:S(2)}) copy-start(f32[3,3,2048]{2,1,0:T(4,128)} %holed_k_ref.3) | copy-start | bytes 221188
  3.1 14.1 %collective-permute-start = (bf16[40,2048]{1,0:T(8,128)(2,1)}, bf16[40,2048]{1,0:T(8,128)(2,1)S(1)}, u32[]{:S(2)}, u32[]{:S(2)}) collective-permute-start(bf16[40,2048]{1,0:T(8,128)(2,1)} %get-tuple-element.16), channel_id=1, source_target_pairs={{0,1},{1,0},{2,3},{3,2},{4,5},{5,4},{6,7},{7,6},{8,9},{9,8},{10,11... | collective-permute-start | bytes 491528 | tf_op jit(solution)/shard_map/ppermute | solution.py:451
  11.8 15.7 %copy-start.2 = (bf16[480,256]{1,0:T(8,128)(2,1)S(1)}, bf16[480,256]{1,0:T(8,128)(2,1)}, u32[]{:S(2)}) copy-start(bf16[480,256]{1,0:T(8,128)(2,1)} %get-tuple-element.18.weighted_ref) | copy-start | bytes 737284
  11.9 15.7 %collective-permute-start.1 = (bf16[480,256]{1,0:T(8,128)(2,1)}, bf16[480,256]{1,0:T(8,128)(2,1)S(1)}, u32[]{:S(2)}, u32[]{:S(2)}) collective-permute-start(bf16[480,256]{1,0:T(8,128)(2,1)} %get-tuple-element.17), channel_id=1, source_target_pairs={{0,3},{1,2},{2,1},{3,0},{4,7},{5,6},{6,5},{7,4},{8,11},{9,10},{10,... | collective-permute-start | bytes 737288 | tf_op jit(solution)/shard_map/ppermute | solution.py:450
  22.6 20.2 %collective-permute-start.2 = (bf16[480,256]{1,0:T(8,128)(2,1)S(1)}, bf16[480,256]{1,0:T(8,128)(2,1)S(1)}, u32[]{:S(2)}, u32[]{:S(2)}) collective-permute-start(bf16[480,256]{1,0:T(8,128)(2,1)S(1)} %get-tuple-element.22), channel_id=1, source_target_pairs={{0,3},{3,0},{4,7},{7,4},{8,11},{11,8},{12,15},{15,12},{16,19},{19,... | collective-permute-start | bytes 737288 | tf_op jit(solution)/shard_map/ppermute | solution.py:454
  89.2 11.3 %all-to-all-start.4 = ((bf16[16,18,8,128]{3,2,1,0:T(8,128)(2,1)}), bf16[16,18,8,128]{3,2,1,0:T(8,128)(2,1)S(1)}, u32[]{:S(2)}, u32[]{:S(2)}) async-start(bf16[16,18,8,128]{3,2,1,0:T(8,128)(2,1)} %broadcast_in_dim.15), calls=%async_computation.4 | async-start | bytes 1179648 | tf_op jit(solution)/shard_map/all_to_all | solution.py:45

commit v3 on v2

--- a/solution.py
+++ b/solution.py
@@ -20,7 +20,8 @@
 PACKED = 256
 LANES = 128
 GRAD_ROWS = 32
-PAYLOAD_ROWS = 2 * CHANNELS + CHANNELS // LANES * GRAD_ROWS
+HALF = CHANNELS // 2
+PAYLOAD_ROWS = 2 * HALF + HALF // LANES * GRAD_ROWS
 F32 = jnp.float32
 BF16 = jnp.bfloat16
 
@@ -242,7 +243,7 @@
         lines += [line(v) for v in own_g]
         lines += [v * down for v in far_lines]
         lines.append(jnp.zeros((GRAD_ROWS - len(lines), LANES), F32))
-        at = 2 * CHANNELS + (step * (BLOCK // LANES) + chunk) * GRAD_ROWS
+        at = 2 * HALF + (step * (BLOCK // LANES) + chunk) * GRAD_ROWS
         payload_ref[pl.ds(pl.multiple_of(at, GRAD_ROWS), GRAD_ROWS), :] = jnp.concatenate(
             lines, 0
         ).astype(BF16)
@@ -251,7 +252,7 @@
     part = lax.dot_general(a_own[...], weighted_ref[...], tn, preferred_element_type=F32)
     part += lax.dot_general(a_far[...], wfar[...], tn, preferred_element_type=F32)
     for half in range(WIDTH // LANES):
-        at = pl.multiple_of(half * CHANNELS + step * BLOCK, BLOCK)
+        at = pl.multiple_of(half * HALF + step * BLOCK, BLOCK)
         payload_ref[pl.ds(at, BLOCK), :] = part[:, half * LANES : (half + 1) * LANES].astype(BF16)
 
     @pl.when(step == pl.num_programs(0) - 1)
@@ -263,12 +264,12 @@
     return pl.BlockSpec(shape, lambda k, s: (0,) * len(shape))
 
 
-def kernel_call(body, in_specs, out_specs, out_shape, scratch_shapes, flops):
+def kernel_call(body, steps, in_specs, out_specs, out_shape, scratch_shapes, flops):
     return pl.pallas_call(
         body,
         grid_spec=pltpu.PrefetchScalarGridSpec(
             num_scalar_prefetch=1,
-            grid=(CHANNELS // BLOCK,),
+            grid=(steps,),
             in_specs=in_specs,
             out_specs=out_specs,
             scratch_shapes=scratch_shapes,
@@ -279,18 +280,25 @@
     )
 
 
-SLAB_SPEC = pl.BlockSpec((ROWS, COLS, BLOCK), lambda k, s: (0, 0, k))
-LINE_SPEC = pl.BlockSpec((COLS, BLOCK), lambda k, s: (0, k))
-TAPS_SPEC = pl.BlockSpec((3, 3, BLOCK), lambda k, s: (0, 0, k))
-POINT_SPEC = pl.BlockSpec((BLOCK, WIDTH), lambda k, s: (k, 0))
+def channel_specs(at):
+    return (
+        pl.BlockSpec((ROWS, COLS, BLOCK), lambda k, s: (0, 0, at(k, s))),
+        pl.BlockSpec((COLS, BLOCK), lambda k, s: (0, at(k, s))),
+        pl.BlockSpec((3, 3, BLOCK), lambda k, s: (0, 0, at(k, s))),
+        pl.BlockSpec((BLOCK, WIDTH), lambda k, s: (at(k, s), 0)),
+    )
+
+
 CELLS_SPEC = whole((CELLS, WIDTH))
 
 
 def first_work(slab, features, near, first_kernel, holed_kernel, point_weight):
+    slab_spec, line_spec, taps_spec, point_spec = channel_specs(lambda k, s: k)
     return kernel_call(
         first_body,
-        [SLAB_SPEC, LINE_SPEC, TAPS_SPEC, TAPS_SPEC, POINT_SPEC],
-        [SLAB_SPEC, CELLS_SPEC],
+        CHANNELS // BLOCK,
+        [slab_spec, line_spec, taps_spec, taps_spec, point_spec],
+        [slab_spec, CELLS_SPEC],
         [
             jax.ShapeDtypeStruct((ROWS, COLS, CHANNELS), BF16),
             jax.ShapeDtypeStruct((CELLS, WIDTH), BF16),
@@ -304,20 +312,26 @@
     )(slab, features, near, first_kernel, holed_kernel, point_weight)
 
 
-def second_work(slab, features, near, partner, weighted, first, first_kernel, holed_kernel, point_weight):
+def second_work(
+    other, slab, features, near, partner, weighted, first, first_kernel, holed_kernel, point_weight
+):
     packs = BLOCK // PACKED
+    steps = HALF // BLOCK
+    at = lambda k, s: k + steps * lax.rem(s[0] + other, 2)
+    slab_spec, line_spec, taps_spec, point_spec = channel_specs(at)
     return kernel_call(
         second_body,
+        steps,
         [
-            SLAB_SPEC,
-            LINE_SPEC,
-            pl.BlockSpec((packs * COLS, PACKED), lambda k, s: (k, 0)),
+            slab_spec,
+            line_spec,
+            pl.BlockSpec((packs * COLS, PACKED), lambda k, s: (at(k, s), 0)),
             CELLS_SPEC,
             CELLS_SPEC,
-            SLAB_SPEC,
-            TAPS_SPEC,
-            TAPS_SPEC,
-            POINT_SPEC,
+            slab_spec,
+            taps_spec,
+            taps_spec,
+            point_spec,
         ],
         [whole((PAYLOAD_ROWS, LANES)), CELLS_SPEC],
         [
@@ -334,7 +348,7 @@
             pltpu.VMEM((COLS, LANES), F32),
             pltpu.VMEM((CELLS, WIDTH), F32),
         ],
-        10 * 2 * CELLS * CHANNELS * WIDTH,
+        1000 * 2 * CELLS * HALF * WIDTH,
     )(
         slab,
         features,
@@ -349,10 +363,9 @@
     )
 
 
-def prepare_body(slab_ref, label_ref, cot_ref, near_ref, far_ref, row_ref, message_ref, weighted_ref):
+def prepare_body(slab_ref, label_ref, cot_ref, far_ref, _, message_ref, weighted_ref):
     slab = slab_ref[0]
     outer = jnp.logical_or(slab == 0, slab == 3)
-    row_ref[...] = near_ref[0]
     diagonal = lax.broadcasted_iota(jnp.int32, (COLS, COLS), 0) == lax.broadcasted_iota(
         jnp.int32, (COLS, COLS), 1
     )
@@ -381,56 +394,44 @@
         message_ref[pl.ds(packs * COLS, rest), :] = jnp.zeros((rest, WIDTH), BF16)
 
 
-def prepare(slab, features, labels, cotangent):
-    def edge_row(far):
-        last = lambda s: (ROWS - 1) * lax.rem(s[0] + 1 - far, 2)
-        return pl.BlockSpec((1, COLS, CHANNELS), lambda k, s: (last(s), 0, 0))
-
+def prepare(slab, features, labels, cotangent, weights):
+    far_row = pl.BlockSpec((1, COLS, CHANNELS), lambda k, s: ((ROWS - 1) * lax.rem(s[0], 2), 0, 0))
     cells = jax.ShapeDtypeStruct((CELLS, WIDTH), BF16)
     return pl.pallas_call(
         prepare_body,
         grid_spec=pltpu.PrefetchScalarGridSpec(
             num_scalar_prefetch=1,
             grid=(1,),
-            in_specs=[whole((ROWS, 1, COLS)), CELLS_SPEC, edge_row(0), edge_row(1)],
-            out_specs=[whole((COLS, CHANNELS)), CELLS_SPEC, CELLS_SPEC],
+            in_specs=[whole((ROWS, 1, COLS)), CELLS_SPEC, far_row, whole((16, WIDTH))],
+            out_specs=[CELLS_SPEC, CELLS_SPEC],
         ),
-        out_shape=[jax.ShapeDtypeStruct((COLS, CHANNELS), BF16), cells, cells],
+        out_shape=[cells, cells],
         compiler_params=pltpu.CompilerParams(vmem_limit_bytes=56 * 2**20),
-    )(slab, labels, cotangent, features, features)
-
-
-def finish_body(left_ref, right_ref, lines_ref, point_ref, first_ref, atrous_ref):
-    point_ref[:, :LANES] = left_ref[...]
-    point_ref[:, LANES:] = right_ref[...]
-
-    @pl.when(pl.program_id(0) == 0)
-    def _():
-        for q in range(CHANNELS // LANES):
-            lanes = pl.ds(q * LANES, LANES)
-            lines = lines_ref[pl.ds(q * GRAD_ROWS, GRAD_ROWS), :].astype(F32)
-            for i in range(3):
-                first_ref[i, :, lanes] = lines[3 * i : 3 * i + 3]
-                atrous_ref[i, :, lanes] = lines[9 + 3 * i : 12 + 3 * i]
+    )(slab, labels, cotangent, features, weights)
+
+
+def finish_body(half_ref, point_ref, first_ref, atrous_ref):
+    point_ref[:, :LANES] = half_ref[:HALF, :]
+    point_ref[:, LANES:] = half_ref[HALF : 2 * HALF, :]
+    for q in range(HALF // LANES):
+        lanes = pl.ds(pl.multiple_of(pl.program_id(0) * HALF + q * LANES, LANES), LANES)
+        lines = half_ref[2 * HALF + q * GRAD_ROWS : 2 * HALF + (q + 1) * GRAD_ROWS, :].astype(F32)
+        for i in range(3):
+            first_ref[i, :, lanes] = lines[3 * i : 3 * i + 3]
+            atrous_ref[i, :, lanes] = lines[9 + 3 * i : 12 + 3 * i]
 
 
 def finish(result):
-    steps = 4
-    block = CHANNELS // steps
     taps_shape = jax.ShapeDtypeStruct((3, 3, CHANNELS), F32)
     taps_spec = pl.BlockSpec((3, 3, CHANNELS), lambda k: (0, 0, 0))
     return pl.pallas_call(
         finish_body,
-        grid=(steps,),
-        in_specs=[
-            pl.BlockSpec((block, LANES), lambda k: (k, 0)),
-            pl.BlockSpec((block, LANES), lambda k: (k + steps, 0)),
-            pl.BlockSpec((block, LANES), lambda k: (2 * steps, 0)),
-        ],
-        out_specs=[pl.BlockSpec((block, WIDTH), lambda k: (k, 0)), taps_spec, taps_spec],
+        grid=(2,),
+        in_specs=[pl.BlockSpec((PAYLOAD_ROWS, LANES), lambda k: (k, 0))],
+        out_specs=[pl.BlockSpec((HALF, WIDTH), lambda k: (k, 0)), taps_spec, taps_spec],
         out_shape=[jax.ShapeDtypeStruct((CHANNELS, WIDTH), BF16), taps_shape, taps_shape],
         compiler_params=pltpu.CompilerParams(vmem_limit_bytes=16 * 2**20),
-    )(result, result, result)
+    )(result)
 
 
 def per_device(features, labels, cotangent, first_kernel, holed_kernel, point_weight):
@@ -443,9 +444,11 @@
     slab = lax.axis_index("slab")
     where = slab[None].astype(jnp.int32)
     feats = features[0]
-    row, message, weighted = prepare(
-        where, feats, labels.reshape(ROWS, 1, COLS), cotangent.reshape(CELLS, WIDTH)
-    )
+    message, weighted = prepare(
+        where, feats, labels.reshape(ROWS, 1, COLS), cotangent.reshape(CELLS, WIDTH), point_weight
+    )
+    spot, message = lax.optimization_barrier((slab, message))
+    row = lax.dynamic_index_in_dim(feats, (ROWS - 1) * (1 - spot % 2), 0, keepdims=False)
     mirrored = [(d, d - d % 4 + 3 - d % 4) for d in range(total)]
     partner = lax.ppermute(message, AXES, mirrored)
     near = lax.ppermute(row, AXES, [(d, d ^ 1) for d in range(total)])
@@ -453,24 +456,24 @@
     first, far = first_work(where, feats, near, first_kernel, holed_kernel, point_weight)
     arrived = lax.ppermute(far, AXES, [pair for pair in mirrored if pair[0] % 4 in (0, 3)])
 
-    payload, own = second_work(
-        where, feats, near, partner, weighted, first, first_kernel, holed_kernel, point_weight
-    )
+    given = (where, feats, near, partner, weighted, first, first_kernel, holed_kernel, point_weight)
+    theirs, own_part = second_work(1, *given)
+    swapped = lax.ppermute(theirs, AXES, [(d, d ^ 1) for d in range(total)])
+    mine, own = second_work(0, *given)
 
     cores = device_groups(dims, "core")
     block = device_groups(dims, "z_low", "x", "y_low")
     z_ring = device_groups(dims, "z_top", "z_mid")
     y_ring = device_groups(dims, "y_high")
-    units = payload.reshape(-1, 8, LANES)
-    units = scattered(units, cores).astype(BF16)
-    units, arrived = lax.optimization_barrier((units, arrived))
+    mine, arrived = lax.optimization_barrier((mine, arrived))
+    units = (mine.astype(F32) + swapped.astype(F32)).astype(BF16).reshape(-1, 8, LANES)
     units = scattered(units, block).astype(BF16)
     units = jnp.sum(gathered(units, z_ring).astype(F32), axis=0).astype(BF16)
     units = (jnp.sum(gathered(units, y_ring).astype(F32), axis=0) * scale).astype(BF16)
     units = gathered(units, block).reshape(-1, 8, LANES)
-    result = gathered(units, cores).reshape(PAYLOAD_ROWS, LANES)
-
-    branch_out = (own + arrived.astype(F32)).astype(BF16).reshape(1, ROWS, COLS, WIDTH)
+    result = gathered(units, cores).reshape(2 * PAYLOAD_ROWS, LANES)
+
+    branch_out = (own_part + own + arrived.astype(F32)).astype(BF16).reshape(1, ROWS, COLS, WIDTH)
     point_grad, first_grad, atrous_grad = finish(result)
     return (branch_out, point_grad, first_grad, atrous_grad)
 

time: 113 us -> 112 us (level)
  blocking collectives: 60 us -> 55.7 us
  starting transfers between devices: 18.3 us -> 21 us
  waiting for transfers between devices: 11.3 us -> 8.94 us
  other arithmetic: 1.47 us -> 3.25 us
    all_to_all x5 -> x4, blocking collectives: 60 us -> 55.7 us  [exchange(): lax.all_to_all(parts, AXES, 0, 0, axis_index_groups=groups, tiled=True)]
    convert_element_type x1 -> x2, other arithmetic: 0.74 us -> 3.11 us  [the longest x1 1.72 us: per_device(): (own_part + own + arrived.astype(F32)).astype(BF16)]
    ppermute x0 -> x1, starting transfers between devices: none -> 1.95 us  [per_device(): swapped = lax.ppermute(theirs, AXES, [(d, d ^ 1) for d in range(total)])]
    ppermute x1, waiting for transfers between devices: 4.27 us -> 2.91 us  [per_device(): partner = lax.ppermute(message, AXES, mirrored)]
    pallas_call x3 -> x4, Pallas kernels: 17.3 us -> 18.6 us  [the longest x2 11.4 us: second_work(): kernel_call(second_body, steps, [slab_spec, line_spec, pl.BlockSpec((pack...]
  transfers between devices with their start and end apart: 4 -> 5, of which waited for: 2 -> 2; matrix products, arithmetic and copies ran while one was open for 1% -> 2% of each run, Pallas kernels for 14% -> 16%
where the time goes in v3:
time: 112 us
  blocking collectives  55.7 us (50%)
  starting transfers between devices  21 us (19%)
  Pallas kernels  20.8 us (19%)
  waiting for transfers between devices  8.94 us (8%)
  other arithmetic  3.25 us (3%)
    all_to_all x4, blocking collectives, exchange(): lax.all_to_all(parts, AXES, 0, 0, axis_index_groups=groups, tiled=True)  55.7 us
    pallas_call x2, Pallas kernels, second_work(): kernel_call(second_body, steps, [slab_spec, line_spec, pl.BlockSpec((pack...  11.4 us
    ppermute x1, starting transfers between devices, per_device(): near = lax.ppermute(row, AXES, [(d, d ^ 1) for d in range(total)])  8.91 us
    pallas_call x1, Pallas kernels, first_work(): kernel_call(first_body, CHANNELS // BLOCK, [slab_spec, line_spec, taps_sp...  6.04 us
    all_to_all x1, waiting for transfers between devices, exchange(): lax.all_to_all(parts, AXES, 0, 0, axis_index_groups=groups, tiled=True)  6.02 us
    ppermute x1, starting transfers between devices, per_device(): partner = lax.ppermute(message, AXES, mirrored)  5.17 us
    all_to_all x1, starting transfers between devices, exchange(): lax.all_to_all(parts, AXES, 0, 0, axis_index_groups=groups, tiled=True)  3.58 us
    ppermute x1, waiting for transfers between devices, per_device(): partner = lax.ppermute(message, AXES, mirrored)  2.91 us
  transfers between devices with their start and end apart: 5, of which 2 were waited for; matrix products, arithmetic and copies ran while one was open for 2% of the time, Pallas kernels for 16%

profile of v3, /device:TPU:1, one launch (start us, length us, event | category | flops | bytes accessed | tf_op | source)
XLA Modules:
  0.0 111.7 jit_solution(9866945189937558882)
XLA Ops:
  0.6 0.0 copy-start
  0.6 0.0 copy-start.1
  0.7 0.0 copy-start.5
  0.7 0.0 copy-start.7
  0.7 2.3 %shard_map.93 = (bf16[480,256]{1,0:T(8,128)(2,1)}, bf16[480,256]{1,0:T(8,128)(2,1)}) custom-call(s32[1]{0:T(128)} %bitcast.slab_ref, s32[12,1,40]{2,1,0:T(1,128)} %bitcast.19, bf16[480,256]{1,0:T(8,128)(2,1)} %bitcast.17, bf16[12,40,2048]{2,1,0:T(8,128)(2,1)} %bitcast.11, bf16[2048,256]{1,0:T(8,128)(2,1)} %point_ref.5), custom_call_target="tpu_custom_call" | custom-call | tf_op jit(solution)/shard_map/pallas_call | solution.py:400
  2.9 0.0 copy-done
  3.0 0.0 copy-start.4
  3.0 0.0 copy-start.6
  3.0 0.0 copy-start.8
  3.0 8.9 %collective-permute-start = (bf16[40,2048]{1,0:T(8,128)(2,1)S(1)}, bf16[40,2048]{1,0:T(8,128)(2,1)S(1)}, u32[]{:S(2)}, u32[]{:S(2)}) collective-permute-start(bf16[40,2048]{1,0:T(8,128)(2,1)S(1)} %dynamic-slice_bitcast_fusion), channel_id=1, source_target_pairs={{0,1},{1,0},{2,3},{3,2},{4,5},{5,4},{6,7},{7,6},{8,9},{9,8},{10,11... | collective-permute-start | bytes 491528 | tf_op jit(solution)/shard_map/ppermute | solution.py:454
  11.9 5.2 %collective-permute-start.1 = (bf16[480,256]{1,0:T(8,128)(2,1)}, bf16[480,256]{1,0:T(8,128)(2,1)S(1)}, u32[]{:S(2)}, u32[]{:S(2)}) collective-permute-start(bf16[480,256]{1,0:T(8,128)(2,1)} %get-tuple-element.21), channel_id=1, source_target_pairs={{0,3},{1,2},{2,1},{3,0},{4,7},{5,6},{6,5},{7,4},{8,11},{9,10},{10,... | collective-permute-start | bytes 737288 | tf_op jit(solution)/shard_map/ppermute | solution.py:453
  17.1 0.0 collective-permute-done.near_ref
  17.1 0.0 copy-done.1
  17.1 0.0 copy-done.5
  17.1 0.0 copy-done.7
  17.1 6.0 %shard_map.94 = (bf16[12,40,2048]{2,1,0:T(8,128)(2,1)S(1)}, bf16[480,256]{1,0:T(8,128)(2,1)}) custom-call(s32[1]{0:T(128)} %bitcast.slab_ref, bf16[12,40,2048]{2,1,0:T(8,128)(2,1)S(1)} %bitcast.12, bf16[40,2048]{1,0:T(8,128)(2,1)S(1)} %collective-permute-done.near_ref, f32[3,3,2048]{2,1,0:T(4,128)S(1)} %copy-done.5, f32[3,3,2048]{2,1,0:T(4,128)S(1)} %copy-done.7, ...), custom_call_target="tpu_custom_call" | custom-call | flops 1006632960 | bytes 8388608 | tf_op jit(solution)/shard_map/pallas_call | solution.py:297
  23.2 1.4 %collective-permute-start.2 = (bf16[480,256]{1,0:T(8,128)(2,1)}, bf16[480,256]{1,0:T(8,128)(2,1)}, u32[]{:S(2)}, u32[]{:S(2)}) collective-permute-start(bf16[480,256]{1,0:T(8,128)(2,1)} %get-tuple-element.27), channel_id=1, source_target_pairs={{0,3},{3,0},{4,7},{7,4},{8,11},{11,8},{12,15},{15,12},{16,19},{19,... | collective-permute-start | bytes 737288 | tf_op jit(solution)/shard_map/ppermute | solution.py:457
  24.5 2.9 %collective-permute-done.1.far_ref.partner_ref = bf16[480,256]{1,0:T(8,128)(2,1)S(1)} collective-permute-done((bf16[480,256]{1,0:T(8,128)(2,1)}, bf16[480,256]{1,0:T(8,128)(2,1)S(1)}, u32[]{:S(2)}, u32[]{:S(2)}) %collective-permute-start.1) | collective-permute-done | bytes 245792 | tf_op jit(solution)/shard_map/ppermute | solution.py:453
  27.5 0.0 copy-done.4
  27.5 0.0 copy-done.6
  27.5 0.0 copy-done.8
  27.5 6.1 %shard_map.95 = (bf16[2304,128]{1,0:T(8,128)(2,1)}, f32[480,256]{1,0:T(8,128)S(1)}) custom-call(s32[1]{0:T(128)} %bitcast.slab_ref, bf16[12,40,2048]{2,1,0:T(8,128)(2,1)S(1)} %bitcast.13, bf16[40,2048]{1,0:T(8,128)(2,1)S(1)} %collective-permute-done.near_ref, bf16[480,256]{1,0:T(8,128)(2,1)S(1)} %collective-permute-done.1.far_ref.partner_ref, ...), custom_call_target="tpu_custom_call" | custom-call | flops 251658240000 | bytes 8388608 | tf_op jit(solution)/shard_map/pallas_call | solution.py:322
  33.6 2.0 %collective-permute-start.3 = (bf16[2304,128]{1,0:T(8,128)(2,1)}, bf16[2304,128]{1,0:T(8,128)(2,1)}, u32[]{:S(2)}, u32[]{:S(2)}) collective-permute-start(bf16[2304,128]{1,0:T(8,128)(2,1)} %get-tuple-element.30), channel_id=1, source_target_pairs={{0,1},{1,0},{2,3},{3,2},{4,5},{5,4},{6,7},{7,6},{8,9},{9,8},{10,11... | collective-permute-start | bytes 1769480 | tf_op jit(solution)/shard_map/ppermute | solution.py:461
  35.5 5.3 %shard_map.96 = (bf16[2304,128]{1,0:T(8,128)(2,1)S(1)}, f32[480,256]{1,0:T(8,128)S(1)}) custom-call(s32[1]{0:T(128)} %bitcast.slab_ref, bf16[12,40,2048]{2,1,0:T(8,128)(2,1)S(1)} %bitcast.14, bf16[40,2048]{1,0:T(8,128)(2,1)S(1)} %collective-permute-done.near_ref, bf16[480,256]{1,0:T(8,128)(2,1)S(1)} %collective-permute-done.1.far_ref.partner_ref, ...), custom_call_target="tpu_custom_call" | custom-call | flops 251658240000 | bytes 8388608 | tf_op jit(solution)/shard_map/pallas_call | solution.py:322
  40.9 0.0 copy-start.2
  40.9 0.0 collective-permute-done.2
  40.9 0.0 collective-permute-done.3
  40.9 1.4 %add_convert_fusion = bf16[2304,128]{1,0:T(8,128)(2,1)S(1)} fusion(bf16[2304,128]{1,0:T(8,128)(2,1)} %collective-permute-done.3, bf16[2304,128]{1,0:T(8,128)(2,1)S(1)} %get-tuple-element.29), kind=kLoop, calls=%fused_computation | loop fusion | flops 1179648 | bytes 1769472 | tf_op jit(solution)/shard_map/convert_element_type | solution.py:469
  42.3 0.0 copy-done.2
  42.3 18.8 %all_to_all.25 = bf16[16,18,8,128]{3,2,1,0:T(8,128)(2,1)S(1)} all-to-all(bf16[16,18,8,128]{3,2,1,0:T(8,128)(2,1)S(1)} %bitcast.16), channel_id=1, replica_groups={{0,4,32,36,64,68,96,100,128,132,160,164,192,196,224,228},{1,5,33,37,65,..., dimensions={0} | all-to-all | bytes 1179648 | tf_op jit(solution)/shard_map/all_to_all | solution.py:46
  61.1 0.1 reduce_sum.33
  61.2 12.7 %all_to_all.26 = bf16[4,18,8,128]{3,2,1,0:T(8,128)(2,1)S(1)} all-to-all(bf16[4,18,8,128]{3,2,1,0:T(8,128)(2,1)S(1)} %broadcast_in_dim.13), channel_id=1, replica_groups={{0,256,2,258},{1,257,3,259},{4,260,6,262},{5,261,7,263},{8,264,10,266},..., dimensions={0} | all-to-all | bytes 294912 | tf_op jit(solution)/shard_map/all_to_all | solution.py:46
  74.0 0.0 copy-start.3
  74.0 13.9 %all_to_all.27 = bf16[4,18,8,128]{3,2,1,0:T(8,128)(2,1)S(1)} all-to-all(bf16[4,18,8,128]{3,2,1,0:T(8,128)(2,1)S(1)} %broadcast_in_dim.14), channel_id=1, replica_groups={{0,8,16,24},{1,9,17,25},{2,10,18,26},{3,11,19,27},{4,12,20,28},{5,13,21..., dimensions={0} | all-to-all | bytes 294912 | tf_op jit(solution)/shard_map/all_to_all | solution.py:46
  87.9 0.9 broadcast_in_dim.15
  88.8 3.6 %all-to-all-start.3 = ((bf16[16,18,8,128]{3,2,1,0:T(8,128)(2,1)}), bf16[16,18,8,128]{3,2,1,0:T(8,128)(2,1)S(1)}, u32[]{:S(2)}, u32[]{:S(2)}) async-start(bf16[16,18,8,128]{3,2,1,0:T(8,128)(2,1)} %broadcast_in_dim.15), calls=%async_computation.3 | async-start | bytes 1179648 | tf_op jit(solution)/shard_map/all_to_all | solution.py:46
  92.4 0.0 copy-done.3
  92.4 1.7 %add_convert_fusion.1 = bf16[480,256]{1,0:T(8,128)(2,1)} fusion(bf16[480,256]{1,0:T(8,128)(2,1)} %collective-permute-done.2, f32[480,256]{1,0:T(8,128)S(1)} %get-tuple-element.24, f32[480,256]{1,0:T(8,128)S(1)} %copy-done.3), kind=kLoop, calls=%fused_computation.1 | loop fusion | flops 491520 | bytes 1474560 | tf_op jit(solution)/shard_map/convert_element_type | solution.py:476
  94.1 6.0 %all-to-all-done.3 = bf16[16,18,8,128]{3,2,1,0:T(8,128)(2,1)S(1)} async-done(((bf16[16,18,8,128]{3,2,1,0:T(8,128)(2,1)}), bf16[16,18,8,128]{3,2,1,0:T(8,128)(2,1)S(1)}, u32[]{:S(2)}, u32[]{:S(2)}) %all-to-all-start.3) | async-done | bytes 589856 | tf_op jit(solution)/shard_map/all_to_all | solution.py:46
  100.1 0.1 broadcast_in_dim.33
  100.2 10.4 %all_to_all.28 = bf16[2,288,8,128]{3,2,1,0:T(8,128)(2,1)S(1)} all-to-all(bf16[2,288,8,128]{3,2,1,0:T(8,128)(2,1)S(1)} %broadcast_in_dim.33), channel_id=1, replica_groups={{0,1},{2,3},{4,5},{6,7},{8,9},{10,11},{12,13},{14,15},{16,17},{18,19},{..., dimensions={0} | all-to-all | bytes 2359296 | tf_op jit(solution)/shard_map/all_to_all | solution.py:46
  110.6 1.1 %shard_map.97 = (bf16[2048,256]{1,0:T(8,128)(2,1)}, f32[3,3,2048]{2,1,0:T(4,128)}, f32[3,3,2048]{2,1,0:T(4,128)}) custom-call(bf16[4608,128]{1,0:T(8,128)(2,1)S(1)} %bitcast.10), custom_call_target="tpu_custom_call" | custom-call | tf_op jit(solution)/shard_map/pallas_call | solution.py:427
  (6 shorter events, 0.1 us)
Async XLA Ops:
  0.6 2.3 %copy-start = (bf16[1,12,40,2048]{3,2,1,0:T(8,128)(2,1)S(1)}, bf16[1,12,40,2048]{3,2,1,0:T(8,128)(2,1)}, u32[]{:S(2)}) copy-start(bf16[1,12,40,2048]{3,2,1,0:T(8,128)(2,1)} %param.6) | copy-start | bytes 5898244
  0.6 16.5 %copy-start.1 = (bf16[2048,256]{1,0:T(8,128)(2,1)S(1)}, bf16[2048,256]{1,0:T(8,128)(2,1)}, u32[]{:S(2)}) copy-start(bf16[2048,256]{1,0:T(8,128)(2,1)} %point_ref.5) | copy-start | bytes 3145732
  0.7 16.5 %copy-start.5 = (f32[3,3,2048]{2,1,0:T(4,128)S(1)}, f32[3,3,2048]{2,1,0:T(4,128)}, u32[]{:S(2)}) copy-start(f32[3,3,2048]{2,1,0:T(4,128)} %first_k_ref.5) | copy-start | bytes 221188
  0.7 16.5 %copy-start.7 = (f32[3,3,2048]{2,1,0:T(4,128)S(1)}, f32[3,3,2048]{2,1,0:T(4,128)}, u32[]{:S(2)}) copy-start(f32[3,3,2048]{2,1,0:T(4,128)} %holed_k_ref.5) | copy-start | bytes 221188
  3.0 24.5 %copy-start.4 = (bf16[480,256]{1,0:T(8,128)(2,1)S(1)}, bf16[480,256]{1,0:T(8,128)(2,1)}, u32[]{:S(2)}) copy-start(bf16[480,256]{1,0:T(8,128)(2,1)} %get-tuple-element.22.weighted_ref) | copy-start | bytes 737284
  3.0 24.5 %copy-start.6 = (f32[3,3,2048]{2,1,0:T(4,128)S(1)}, f32[3,3,2048]{2,1,0:T(4,128)}, u32[]{:S(2)}) copy-start(f32[3,3,2048]{2,1,0:T(4,128)} %first_k_ref.5) | copy-start | bytes 221188
  3.0 24.5 %copy-start.8 = (f32[3,3,2048]{2,1,0:T(4,128)S(1)}, f32[3,3,2048]{2,1,0:T(4,128)}, u32[]{:S(2)}) copy-start(f32[3,3,2048]{2,1,0:T(4,128)} %holed_k_ref.5) | copy-start | bytes 221188
  3.0 14.1 %collective-permute-start = (bf16[40,2048]{1,0:T(8,128)(2,1)S(1)}, bf16[40,2048]{1,0:T(8,128)(2,1)S(1)}, u32[]{:S(2)}, u32[]{:S(2)}) collective-permute-start(bf16[40,2048]{1,0:T(8,128)(2,1)S(1)} %dynamic-slice_bitcast_fusion), channel_id=1, source_target_pairs={{0,1},{1,0},{2,3},{3,2},{4,5},{5,4},{6,7},{7,6},{8,9},{9,8},{10,11... | collective-permute-start | bytes 491528 | tf_op jit(solution)/shard_map/ppermute | solution.py:454
  11.9 15.5 %collective-permute-start.1 = (bf16[480,256]{1,0:T(8,128)(2,1)}, bf16[480,256]{1,0:T(8,128)(2,1)S(1)}, u32[]{:S(2)}, u32[]{:S(2)}) collective-permute-start(bf16[480,256]{1,0:T(8,128)(2,1)} %get-tuple-element.21), channel_id=1, source_target_pairs={{0,3},{1,2},{2,1},{3,0},{4,7},{5,6},{6,5},{7,4},{8,11},{9,10},{10,... | collective-permute-start | bytes 737288 | tf_op jit(solution)/shard_map/ppermute | solution.py:453
  23.2 17.7 %collective-permute-start.2 = (bf16[480,256]{1,0:T(8,128)(2,1)}, bf16[480,256]{1,0:T(8,128)(2,1)}, u32[]{:S(2)}, u32[]{:S(2)}) collective-permute-start(bf16[480,256]{1,0:T(8,128)(2,1)} %get-tuple-element.27), channel_id=1, source_target_pairs={{0,3},{3,0},{4,7},{7,4},{8,11},{11,8},{12,15},{15,12},{16,19},{19,... | collective-permute-start | bytes 737288 | tf_op jit(solution)/shard_map/ppermute | solution.py:457
  33.6 7.3 %collective-permute-start.3 = (bf16[2304,128]{1,0:T(8,128)(2,1)}, bf16[2304,128]{1,0:T(8,128)(2,1)}, u32[]{:S(2)}, u32[]{:S(2)}) collective-permute-start(bf16[2304,128]{1,0:T(8,128)(2,1)} %get-tuple-element.30), channel_id=1, source_target_pairs={{0,1},{1,0},{2,3},{3,2},{4,5},{5,4},{6,7},{7,6},{8,9},{9,8},{10,11... | collective-permute-start | bytes 1769480 | tf_op jit(solution)/shard_map/ppermute | solution.py:461
  40.9 1.4 %copy-start.2 = (f32[480,256]{1,0:T(8,128)}, f32[480,256]{1,0:T(8,128)S(1)}, u32[]{:S(2)}) copy-start(f32[480,256]{1,0:T(8,128)S(1)} %get-tuple-element.25) | copy-start | bytes 1474564
  74.0 18.4 %copy-start.3 = (f32[480,256]{1,0:T(8,128)S(1)}, f32[480,256]{1,0:T(8,128)}, u32[]{:S(2)}) copy-start(f32[480,256]{1,0:T(8,128)} %copy-done.2) | copy-start | bytes 1474564
  88.8 11.3 %all-to-all-start.3 = ((bf16[16,18,8,128]{3,2,1,0:T(8,128)(2,1)}), bf16[16,18,8,128]{3,2,1,0:T(8,128)(2,1)S(1)}, u32[]{:S(2)}, u32[]{:S(2)}) async-start(bf16[16,18,8,128]{3,2,1,0:T(8,128)(2,1)} %broadcast_in_dim.15), calls=%async_computation.3 | async-start | bytes 1179648 | tf_op jit(solution)/shard_map/all_to_all | solution.py:46

commit v4 on v3

--- a/solution.py
+++ b/solution.py
@@ -205,6 +205,7 @@
         f_edge[...] = conv_row(fk, x).astype(BF16).astype(F32)
 
         zero = jnp.zeros((8, LANES), F32)
+        is_low = lax.broadcasted_iota(jnp.int32, (8, LANES), 0) < EDGE
         first_acc, own_g, far_g = [zero] * 9, [zero] * 3, [zero] * 3
         for p in range(ROWS // 2):
             base = p * 2 * COLS
@@ -222,8 +223,12 @@
                     sums[0] += f_ends[1] * b[COLS - 8 :]
                     sums[1] += fold(f * b)
                     sums[2] += f_ends[0] * b[:8]
-                bo_ends, bf_ends = ends(bo), ends(bf)
-                g = spread(mk[::-1], bo, bo_ends) + spread(kf[::-1], bf, bf_ends)
+                g = mk[1] * bo + kf[1] * bf
+                high = mk[0] * bo[COLS - 8 :] + kf[0] * bf[COLS - 8 :]
+                low = mk[2] * bo[:8] + kf[2] * bf[:8]
+                high = jnp.where(is_low, pltpu.roll(high, 4, 0), 0.0)
+                low = jnp.where(is_low, 0.0, pltpu.roll(low, 4, 0))
+                g = jnp.concatenate([g[:8] + high, g[8 : COLS - 8], g[COLS - 8 :] + low], 0)
                 g = g.astype(BF16).astype(F32)
                 shifted = [from_right(g), g, from_left(g)]
                 for i in range(3):

time: 112 us -> 112 us (level)
  no operation moved by 1% of the time
where the time goes in v4:
time: 112 us
  blocking collectives  55.8 us (50%)
  starting transfers between devices  21 us (19%)
  Pallas kernels  20.7 us (18%)
  waiting for transfers between devices  8.94 us (8%)
  other arithmetic  3.25 us (3%)
    all_to_all x4, blocking collectives, exchange(): lax.all_to_all(parts, AXES, 0, 0, axis_index_groups=groups, tiled=True)  55.8 us
    pallas_call x2, Pallas kernels, second_work(): kernel_call(second_body, steps, [slab_spec, line_spec, pl.BlockSpec((pack...  11.3 us
    ppermute x1, starting transfers between devices, per_device(): near = lax.ppermute(row, AXES, [(d, d ^ 1) for d in range(total)])  8.91 us
    pallas_call x1, Pallas kernels, first_work(): kernel_call(first_body, CHANNELS // BLOCK, [slab_spec, line_spec, taps_sp...  6.04 us
    all_to_all x1, waiting for transfers between devices, exchange(): lax.all_to_all(parts, AXES, 0, 0, axis_index_groups=groups, tiled=True)  6.02 us
    ppermute x1, starting transfers between devices, per_device(): partner = lax.ppermute(message, AXES, mirrored)  5.17 us
    all_to_all x1, starting transfers between devices, exchange(): lax.all_to_all(parts, AXES, 0, 0, axis_index_groups=groups, tiled=True)  3.58 us
    ppermute x1, waiting for transfers between devices, per_device(): partner = lax.ppermute(message, AXES, mirrored)  2.91 us
  transfers between devices with their start and end apart: 5, of which 2 were waited for; matrix products, arithmetic and copies ran while one was open for 2% of the time, Pallas kernels for 16%

profile of v4, /device:TPU:1, one launch (start us, length us, event | category | flops | bytes accessed | tf_op | source)
XLA Modules:
  0.0 111.6 jit_solution(7184511682940947486)
XLA Ops:
  0.6 0.0 copy-start
  0.6 0.0 copy-start.1
  0.7 0.0 copy-start.5
  0.7 0.0 copy-start.7
  0.7 2.3 %shard_map.93 = (bf16[480,256]{1,0:T(8,128)(2,1)}, bf16[480,256]{1,0:T(8,128)(2,1)}) custom-call(s32[1]{0:T(128)} %bitcast.slab_ref, s32[12,1,40]{2,1,0:T(1,128)} %bitcast.19, bf16[480,256]{1,0:T(8,128)(2,1)} %bitcast.17, bf16[12,40,2048]{2,1,0:T(8,128)(2,1)} %bitcast.11, bf16[2048,256]{1,0:T(8,128)(2,1)} %point_ref.5), custom_call_target="tpu_custom_call" | custom-call | tf_op jit(solution)/shard_map/pallas_call | solution.py:405
  2.9 0.0 copy-done
  3.0 0.0 copy-start.4
  3.0 0.0 copy-start.6
  3.0 0.0 copy-start.8
  3.0 8.9 %collective-permute-start = (bf16[40,2048]{1,0:T(8,128)(2,1)S(1)}, bf16[40,2048]{1,0:T(8,128)(2,1)S(1)}, u32[]{:S(2)}, u32[]{:S(2)}) collective-permute-start(bf16[40,2048]{1,0:T(8,128)(2,1)S(1)} %dynamic-slice_bitcast_fusion), channel_id=1, source_target_pairs={{0,1},{1,0},{2,3},{3,2},{4,5},{5,4},{6,7},{7,6},{8,9},{9,8},{10,11... | collective-permute-start | bytes 491528 | tf_op jit(solution)/shard_map/ppermute | solution.py:459
  11.9 5.2 %collective-permute-start.1 = (bf16[480,256]{1,0:T(8,128)(2,1)}, bf16[480,256]{1,0:T(8,128)(2,1)S(1)}, u32[]{:S(2)}, u32[]{:S(2)}) collective-permute-start(bf16[480,256]{1,0:T(8,128)(2,1)} %get-tuple-element.21), channel_id=1, source_target_pairs={{0,3},{1,2},{2,1},{3,0},{4,7},{5,6},{6,5},{7,4},{8,11},{9,10},{10,... | collective-permute-start | bytes 737288 | tf_op jit(solution)/shard_map/ppermute | solution.py:458
  17.1 0.0 collective-permute-done.near_ref
  17.1 0.0 copy-done.1
  17.1 0.0 copy-done.5
  17.1 0.0 copy-done.7
  17.1 6.0 %shard_map.94 = (bf16[12,40,2048]{2,1,0:T(8,128)(2,1)S(1)}, bf16[480,256]{1,0:T(8,128)(2,1)}) custom-call(s32[1]{0:T(128)} %bitcast.slab_ref, bf16[12,40,2048]{2,1,0:T(8,128)(2,1)S(1)} %bitcast.12, bf16[40,2048]{1,0:T(8,128)(2,1)S(1)} %collective-permute-done.near_ref, f32[3,3,2048]{2,1,0:T(4,128)S(1)} %copy-done.5, f32[3,3,2048]{2,1,0:T(4,128)S(1)} %copy-done.7, ...), custom_call_target="tpu_custom_call" | custom-call | flops 1006632960 | bytes 8388608 | tf_op jit(solution)/shard_map/pallas_call | solution.py:302
  23.2 1.4 %collective-permute-start.2 = (bf16[480,256]{1,0:T(8,128)(2,1)}, bf16[480,256]{1,0:T(8,128)(2,1)}, u32[]{:S(2)}, u32[]{:S(2)}) collective-permute-start(bf16[480,256]{1,0:T(8,128)(2,1)} %get-tuple-element.27), channel_id=1, source_target_pairs={{0,3},{3,0},{4,7},{7,4},{8,11},{11,8},{12,15},{15,12},{16,19},{19,... | collective-permute-start | bytes 737288 | tf_op jit(solution)/shard_map/ppermute | solution.py:462
  24.5 2.9 %collective-permute-done.1.far_ref.partner_ref = bf16[480,256]{1,0:T(8,128)(2,1)S(1)} collective-permute-done((bf16[480,256]{1,0:T(8,128)(2,1)}, bf16[480,256]{1,0:T(8,128)(2,1)S(1)}, u32[]{:S(2)}, u32[]{:S(2)}) %collective-permute-start.1) | collective-permute-done | bytes 245792 | tf_op jit(solution)/shard_map/ppermute | solution.py:458
  27.5 0.0 copy-done.4
  27.5 0.0 copy-done.6
  27.5 0.0 copy-done.8
  27.5 6.1 %shard_map.95 = (bf16[2304,128]{1,0:T(8,128)(2,1)}, f32[480,256]{1,0:T(8,128)S(1)}) custom-call(s32[1]{0:T(128)} %bitcast.slab_ref, bf16[12,40,2048]{2,1,0:T(8,128)(2,1)S(1)} %bitcast.13, bf16[40,2048]{1,0:T(8,128)(2,1)S(1)} %collective-permute-done.near_ref, bf16[480,256]{1,0:T(8,128)(2,1)S(1)} %collective-permute-done.1.far_ref.partner_ref, ...), custom_call_target="tpu_custom_call" | custom-call | flops 251658240000 | bytes 8388608 | tf_op jit(solution)/shard_map/pallas_call | solution.py:327
  33.5 2.0 %collective-permute-start.3 = (bf16[2304,128]{1,0:T(8,128)(2,1)}, bf16[2304,128]{1,0:T(8,128)(2,1)}, u32[]{:S(2)}, u32[]{:S(2)}) collective-permute-start(bf16[2304,128]{1,0:T(8,128)(2,1)} %get-tuple-element.30), channel_id=1, source_target_pairs={{0,1},{1,0},{2,3},{3,2},{4,5},{5,4},{6,7},{7,6},{8,9},{9,8},{10,11... | collective-permute-start | bytes 1769480 | tf_op jit(solution)/shard_map/ppermute | solution.py:466
  35.5 5.2 %shard_map.96 = (bf16[2304,128]{1,0:T(8,128)(2,1)S(1)}, f32[480,256]{1,0:T(8,128)S(1)}) custom-call(s32[1]{0:T(128)} %bitcast.slab_ref, bf16[12,40,2048]{2,1,0:T(8,128)(2,1)S(1)} %bitcast.14, bf16[40,2048]{1,0:T(8,128)(2,1)S(1)} %collective-permute-done.near_ref, bf16[480,256]{1,0:T(8,128)(2,1)S(1)} %collective-permute-done.1.far_ref.partner_ref, ...), custom_call_target="tpu_custom_call" | custom-call | flops 251658240000 | bytes 8388608 | tf_op jit(solution)/shard_map/pallas_call | solution.py:327
  40.7 0.0 copy-start.2
  40.7 0.0 collective-permute-done.2
  40.8 0.0 collective-permute-done.3
  40.8 1.4 %add_convert_fusion = bf16[2304,128]{1,0:T(8,128)(2,1)S(1)} fusion(bf16[2304,128]{1,0:T(8,128)(2,1)} %collective-permute-done.3, bf16[2304,128]{1,0:T(8,128)(2,1)S(1)} %get-tuple-element.29), kind=kLoop, calls=%fused_computation | loop fusion | flops 1179648 | bytes 1769472 | tf_op jit(solution)/shard_map/convert_element_type | solution.py:474
  42.2 0.0 copy-done.2
  42.2 18.8 %all_to_all.25 = bf16[16,18,8,128]{3,2,1,0:T(8,128)(2,1)S(1)} all-to-all(bf16[16,18,8,128]{3,2,1,0:T(8,128)(2,1)S(1)} %bitcast.16), channel_id=1, replica_groups={{0,4,32,36,64,68,96,100,128,132,160,164,192,196,224,228},{1,5,33,37,65,..., dimensions={0} | all-to-all | bytes 1179648 | tf_op jit(solution)/shard_map/all_to_all | solution.py:46
  60.9 0.1 reduce_sum.33
  61.0 12.7 %all_to_all.26 = bf16[4,18,8,128]{3,2,1,0:T(8,128)(2,1)S(1)} all-to-all(bf16[4,18,8,128]{3,2,1,0:T(8,128)(2,1)S(1)} %broadcast_in_dim.13), channel_id=1, replica_groups={{0,256,2,258},{1,257,3,259},{4,260,6,262},{5,261,7,263},{8,264,10,266},..., dimensions={0} | all-to-all | bytes 294912 | tf_op jit(solution)/shard_map/all_to_all | solution.py:46
  73.8 0.0 copy-start.3
  73.9 13.9 %all_to_all.27 = bf16[4,18,8,128]{3,2,1,0:T(8,128)(2,1)S(1)} all-to-all(bf16[4,18,8,128]{3,2,1,0:T(8,128)(2,1)S(1)} %broadcast_in_dim.14), channel_id=1, replica_groups={{0,8,16,24},{1,9,17,25},{2,10,18,26},{3,11,19,27},{4,12,20,28},{5,13,21..., dimensions={0} | all-to-all | bytes 294912 | tf_op jit(solution)/shard_map/all_to_all | solution.py:46
  87.8 0.9 broadcast_in_dim.15
  88.7 3.6 %all-to-all-start.3 = ((bf16[16,18,8,128]{3,2,1,0:T(8,128)(2,1)}), bf16[16,18,8,128]{3,2,1,0:T(8,128)(2,1)S(1)}, u32[]{:S(2)}, u32[]{:S(2)}) async-start(bf16[16,18,8,128]{3,2,1,0:T(8,128)(2,1)} %broadcast_in_dim.15), calls=%async_computation.3 | async-start | bytes 1179648 | tf_op jit(solution)/shard_map/all_to_all | solution.py:46
  92.3 0.0 copy-done.3
  92.3 1.7 %add_convert_fusion.1 = bf16[480,256]{1,0:T(8,128)(2,1)} fusion(bf16[480,256]{1,0:T(8,128)(2,1)} %collective-permute-done.2, f32[480,256]{1,0:T(8,128)S(1)} %get-tuple-element.24, f32[480,256]{1,0:T(8,128)S(1)} %copy-done.3), kind=kLoop, calls=%fused_computation.1 | loop fusion | flops 491520 | bytes 1474560 | tf_op jit(solution)/shard_map/convert_element_type | solution.py:481
  94.0 6.0 %all-to-all-done.3 = bf16[16,18,8,128]{3,2,1,0:T(8,128)(2,1)S(1)} async-done(((bf16[16,18,8,128]{3,2,1,0:T(8,128)(2,1)}), bf16[16,18,8,128]{3,2,1,0:T(8,128)(2,1)S(1)}, u32[]{:S(2)}, u32[]{:S(2)}) %all-to-all-start.3) | async-done | bytes 589856 | tf_op jit(solution)/shard_map/all_to_all | solution.py:46
  100.0 0.1 broadcast_in_dim.33
  100.1 10.4 %all_to_all.28 = bf16[2,288,8,128]{3,2,1,0:T(8,128)(2,1)S(1)} all-to-all(bf16[2,288,8,128]{3,2,1,0:T(8,128)(2,1)S(1)} %broadcast_in_dim.33), channel_id=1, replica_groups={{0,1},{2,3},{4,5},{6,7},{8,9},{10,11},{12,13},{14,15},{16,17},{18,19},{..., dimensions={0} | all-to-all | bytes 2359296 | tf_op jit(solution)/shard_map/all_to_all | solution.py:46
  110.5 1.1 %shard_map.97 = (bf16[2048,256]{1,0:T(8,128)(2,1)}, f32[3,3,2048]{2,1,0:T(4,128)}, f32[3,3,2048]{2,1,0:T(4,128)}) custom-call(bf16[4608,128]{1,0:T(8,128)(2,1)S(1)} %bitcast.10), custom_call_target="tpu_custom_call" | custom-call | tf_op jit(solution)/shard_map/pallas_call | solution.py:432
  (6 shorter events, 0.1 us)
Async XLA Ops:
  0.6 2.3 %copy-start = (bf16[1,12,40,2048]{3,2,1,0:T(8,128)(2,1)S(1)}, bf16[1,12,40,2048]{3,2,1,0:T(8,128)(2,1)}, u32[]{:S(2)}) copy-start(bf16[1,12,40,2048]{3,2,1,0:T(8,128)(2,1)} %param.6) | copy-start | bytes 5898244
  0.6 16.5 %copy-start.1 = (bf16[2048,256]{1,0:T(8,128)(2,1)S(1)}, bf16[2048,256]{1,0:T(8,128)(2,1)}, u32[]{:S(2)}) copy-start(bf16[2048,256]{1,0:T(8,128)(2,1)} %point_ref.5) | copy-start | bytes 3145732
  0.7 16.5 %copy-start.5 = (f32[3,3,2048]{2,1,0:T(4,128)S(1)}, f32[3,3,2048]{2,1,0:T(4,128)}, u32[]{:S(2)}) copy-start(f32[3,3,2048]{2,1,0:T(4,128)} %first_k_ref.5) | copy-start | bytes 221188
  0.7 16.5 %copy-start.7 = (f32[3,3,2048]{2,1,0:T(4,128)S(1)}, f32[3,3,2048]{2,1,0:T(4,128)}, u32[]{:S(2)}) copy-start(f32[3,3,2048]{2,1,0:T(4,128)} %holed_k_ref.5) | copy-start | bytes 221188
  3.0 24.5 %copy-start.4 = (bf16[480,256]{1,0:T(8,128)(2,1)S(1)}, bf16[480,256]{1,0:T(8,128)(2,1)}, u32[]{:S(2)}) copy-start(bf16[480,256]{1,0:T(8,128)(2,1)} %get-tuple-element.22.weighted_ref) | copy-start | bytes 737284
  3.0 24.5 %copy-start.6 = (f32[3,3,2048]{2,1,0:T(4,128)S(1)}, f32[3,3,2048]{2,1,0:T(4,128)}, u32[]{:S(2)}) copy-start(f32[3,3,2048]{2,1,0:T(4,128)} %first_k_ref.5) | copy-start | bytes 221188
  3.0 24.5 %copy-start.8 = (f32[3,3,2048]{2,1,0:T(4,128)S(1)}, f32[3,3,2048]{2,1,0:T(4,128)}, u32[]{:S(2)}) copy-start(f32[3,3,2048]{2,1,0:T(4,128)} %holed_k_ref.5) | copy-start | bytes 221188
  3.0 14.1 %collective-permute-start = (bf16[40,2048]{1,0:T(8,128)(2,1)S(1)}, bf16[40,2048]{1,0:T(8,128)(2,1)S(1)}, u32[]{:S(2)}, u32[]{:S(2)}) collective-permute-start(bf16[40,2048]{1,0:T(8,128)(2,1)S(1)} %dynamic-slice_bitcast_fusion), channel_id=1, source_target_pairs={{0,1},{1,0},{2,3},{3,2},{4,5},{5,4},{6,7},{7,6},{8,9},{9,8},{10,11... | collective-permute-start | bytes 491528 | tf_op jit(solution)/shard_map/ppermute | solution.py:459
  11.9 15.5 %collective-permute-start.1 = (bf16[480,256]{1,0:T(8,128)(2,1)}, bf16[480,256]{1,0:T(8,128)(2,1)S(1)}, u32[]{:S(2)}, u32[]{:S(2)}) collective-permute-start(bf16[480,256]{1,0:T(8,128)(2,1)} %get-tuple-element.21), channel_id=1, source_target_pairs={{0,3},{1,2},{2,1},{3,0},{4,7},{5,6},{6,5},{7,4},{8,11},{9,10},{10,... | collective-permute-start | bytes 737288 | tf_op jit(solution)/shard_map/ppermute | solution.py:458
  23.2 17.6 %collective-permute-start.2 = (bf16[480,256]{1,0:T(8,128)(2,1)}, bf16[480,256]{1,0:T(8,128)(2,1)}, u32[]{:S(2)}, u32[]{:S(2)}) collective-permute-start(bf16[480,256]{1,0:T(8,128)(2,1)} %get-tuple-element.27), channel_id=1, source_target_pairs={{0,3},{3,0},{4,7},{7,4},{8,11},{11,8},{12,15},{15,12},{16,19},{19,... | collective-permute-start | bytes 737288 | tf_op jit(solution)/shard_map/ppermute | solution.py:462
  33.5 7.2 %collective-permute-start.3 = (bf16[2304,128]{1,0:T(8,128)(2,1)}, bf16[2304,128]{1,0:T(8,128)(2,1)}, u32[]{:S(2)}, u32[]{:S(2)}) collective-permute-start(bf16[2304,128]{1,0:T(8,128)(2,1)} %get-tuple-element.30), channel_id=1, source_target_pairs={{0,1},{1,0},{2,3},{3,2},{4,5},{5,4},{6,7},{7,6},{8,9},{9,8},{10,11... | collective-permute-start | bytes 1769480 | tf_op jit(solution)/shard_map/ppermute | solution.py:466
  40.7 1.4 %copy-start.2 = (f32[480,256]{1,0:T(8,128)}, f32[480,256]{1,0:T(8,128)S(1)}, u32[]{:S(2)}) copy-start(f32[480,256]{1,0:T(8,128)S(1)} %get-tuple-element.25) | copy-start | bytes 1474564
  73.8 18.4 %copy-start.3 = (f32[480,256]{1,0:T(8,128)S(1)}, f32[480,256]{1,0:T(8,128)}, u32[]{:S(2)}) copy-start(f32[480,256]{1,0:T(8,128)} %copy-done.2) | copy-start | bytes 1474564
  88.7 11.3 %all-to-all-start.3 = ((bf16[16,18,8,128]{3,2,1,0:T(8,128)(2,1)}), bf16[16,18,8,128]{3,2,1,0:T(8,128)(2,1)S(1)}, u32[]{:S(2)}, u32[]{:S(2)}) async-start(bf16[16,18,8,128]{3,2,1,0:T(8,128)(2,1)} %broadcast_in_dim.15), calls=%async_computation.3 | async-start | bytes 1179648 | tf_op jit(solution)/shard_map/all_to_all | solution.py:46
